TPU v7x, 32 devices: a whole 2x2x4 slice. The times are simulated.
32 devices in a mesh: parts: 2 (over y), gx: 4 (over z), gy: 2 (over x), gz: 2 (over core).
Axes of the slice: x: 2, y: 2, z: 4, core: 2. Of those that a mesh axis runs over, the one named last changes fastest.
Arguments:
- positions: float32 [8, 2, 2, 3, 256], P(('parts', 'gx'), 'gy', 'gz'), parts along dimension 0, may hold values from 0 to 94
- species: int32 [8, 2, 2, 256], P(('parts', 'gx'), 'gy', 'gz'), parts along dimension 0, may hold values from 0 to 4
- neighbors: int32 [8, 2, 2, 32, 256], P(('parts', 'gx'), 'gy', 'gz'), parts along dimension 0, may hold values from -1 to 6911, as said below
- migration: int32 [8, 2, 2, 32], P(('parts', 'gx'), 'gy', 'gz'), parts along dimension 0, may hold values from -1 to 63, as said below
- latents: bfloat16 [8, 2, 2, 32, 256, 256], P(('parts', 'gx'), 'gy', 'gz'), parts along dimension 0, may hold values from -6 to 6
- w_latent: bfloat16 [256, 384], replicated, may hold values from -0.375 to 0.375
- w_tensor: bfloat16 [192, 256], replicated, may hold values from -0.4375 to 0.4375
- w_radial: float32 [8, 256], replicated, may hold values from -4 to 4
- species_center: float32 [5, 256], replicated, may hold values from -5 to 5
- species_neighbor: float32 [5, 256], replicated, may hold values from -5 to 5
- w_hidden: bfloat16 [256, 256], replicated, may hold values from -0.375 to 0.375
- w_update: bfloat16 [256, 256], replicated, may hold values from -0.375 to 0.375
- w_out: bfloat16 [256], replicated, may hold values from -0.375 to 0.375
Outputs:
- forces: float32 [8, 2, 2, 3, 128], P(('parts', 'gx'), 'gy', 'gz'), parts along dimension 0
- atom_energy: bfloat16 [8, 2, 2, 256], P(('parts', 'gx'), 'gy', 'gz'), parts along dimension 0
- latent_grad: bfloat16 [8, 2, 2, 32, 256, 256], P(('parts', 'gx'), 'gy', 'gz'), parts along dimension 0
There are 2 independent parts, one for each index of `parts`. A program takes and returns all parts, laid end to end along the dimension named above; an argument that names none is the same for every part. Nothing has to cross between parts.
Inputs may be any that keep to these rules, and one draw needn't show every extreme that they name: `neighbors`: A home block is live where its migration entry is not -1. Entries of live centers name atoms of live blocks of devices inside the grid, never the center itself; centers in blocks that are not live have only -1. `migration`: -1 marks a block that is not live; w * 16 + s sends the block to slot s of the device with gx index w and the same gy and gz indices. Every slot of every device receives exactly one block. A device sends at most 8 blocks to one gx index; in every draw some device has all 32 blocks live and sends exactly 8 to every gx index.
All inputs are finite; a program needn't handle non-finite values.
Results may differ from a plain program's by a relative error of at most 0.01.
Values may be sent and summed in bfloat16 or wider, within the bound.
A program may use at most 128 MiB of HBM per device.

v0:
```python
import jax
import jax.numpy as jnp
from jax import lax
from jax.sharding import PartitionSpec as P

NB = 8
CB = 8
K = 32


cutoff_radius = 6.0
sqrt_three = 3.0**0.5
sqrt_five = 5.0**0.5
sqrt_fifteen = 15.0**0.5


def with_halo(cells, sides, width):
    for axis, dim in sides:
        count = lax.axis_size(axis)
        ends = count - 1
        head = lax.slice_in_dim(cells, 0, width, axis=dim)
        tail = lax.slice_in_dim(cells, cells.shape[dim] - width, cells.shape[dim], axis=dim)
        cells = jnp.concatenate(
            [
                lax.ppermute(tail, axis, [(i, (i + 1) % count) for i in range(ends)]),
                cells,
                lax.ppermute(head, axis, [((i + 1) % count, i) for i in range(ends)]),
            ],
            axis=dim,
        )
    return cells


def edge_features(vectors):
    square = jnp.sum(vectors * vectors, axis=0)
    length = jnp.sqrt(square)
    unit_x = vectors[0] / length
    unit_y = vectors[1] / length
    unit_z = vectors[2] / length
    envelope = jnp.maximum(1.0 - square / (cutoff_radius * cutoff_radius), 0.0) ** 2
    harmonics = jnp.stack(
        [
            jnp.ones_like(length),
            sqrt_three * unit_x,
            sqrt_three * unit_y,
            sqrt_three * unit_z,
            sqrt_fifteen * unit_x * unit_y,
            sqrt_fifteen * unit_y * unit_z,
            0.5 * sqrt_five * (3.0 * unit_z * unit_z - 1.0),
            sqrt_fifteen * unit_x * unit_z,
            0.5 * sqrt_fifteen * (unit_x * unit_x - unit_y * unit_y),
        ]
    )
    orders = jnp.arange(1, NB + 1, dtype=jnp.int32).astype(vectors.dtype)
    radial = (2.0 / cutoff_radius) ** 0.5 * jnp.sin(
        orders[:, None] * jnp.pi * length[None, :] / cutoff_radius
    )
    radial = radial / length[None, :] * envelope[None, :]
    return jnp.concatenate([harmonics, radial, envelope[None, :]], axis=0)


def latent_energy(features, latent_wide, species_codes, weights):
    w_latent, w_tensor, w_radial, species_center, species_neighbor, w_hidden, w_update, w_out = (
        weights
    )
    channels = w_tensor.shape[0] // 3
    basis_count = w_radial.shape[0]
    species_count = species_center.shape[0]
    edge_count = latent_wide.shape[0]
    atom_count = edge_count // K
    harmonics = features[:9].T
    radial = features[9 : 9 + basis_count].T
    envelope = features[9 + basis_count]
    latent_low = latent_wide.astype(jnp.bfloat16)
    projected = jnp.dot(latent_low, w_latent, preferred_element_type=jnp.float32)
    env_weight = projected[:, :channels] * envelope[:, None]
    value_weight = projected[:, channels : 2 * channels]
    latent_part = projected[:, 2 * channels :]
    harm_atoms = harmonics.reshape(atom_count, K, 9)
    environment = (
        jnp.einsum(
            "akc,akm->acm",
            env_weight.reshape(atom_count, K, channels),
            harm_atoms,
            precision=lax.Precision.HIGHEST,
        )
        / K**0.5
    )
    pieces = []
    for first_m, last_m in ((0, 1), (1, 4), (4, 9)):
        env_along = jnp.einsum(
            "akm,acm->akc",
            harm_atoms[:, :, first_m:last_m],
            environment[:, :, first_m:last_m],
            precision=lax.Precision.HIGHEST,
        )
        pieces.append(value_weight * env_along.reshape(edge_count, channels))
    invariants = jnp.concatenate(pieces, axis=1).astype(jnp.bfloat16)
    kinds = jnp.arange(species_count, dtype=jnp.int32).astype(species_codes.dtype)
    center_hot = (species_codes[0][:, None] == kinds[None, :]).astype(jnp.float32)
    neighbour_hot = (species_codes[1][:, None] == kinds[None, :]).astype(jnp.float32)
    preact = latent_part + jnp.dot(invariants, w_tensor, preferred_element_type=jnp.float32)
    preact = preact + jnp.dot(radial, w_radial, precision=lax.Precision.HIGHEST)
    preact = preact + jnp.dot(center_hot, species_center, precision=lax.Precision.HIGHEST)
    preact = preact + jnp.dot(neighbour_hot, species_neighbor, precision=lax.Precision.HIGHEST)
    hidden_one = jax.nn.silu(preact).astype(jnp.bfloat16)
    hidden_two = jax.nn.silu(
        jnp.dot(hidden_one, w_hidden, preferred_element_type=jnp.float32)
    ).astype(jnp.bfloat16)
    updated = (
        latent_wide
        + jnp.dot(hidden_two, w_update, preferred_element_type=jnp.float32) * envelope[:, None]
    )
    energy = (
        jnp.dot(updated.astype(jnp.bfloat16), w_out, preferred_element_type=jnp.float32) * envelope
    )
    return jnp.sum(energy.reshape(atom_count, K), axis=1)


def run_blocks(feature_low, species_codes, latent_block, weights):
    features = lax.optimization_barrier(feature_low).astype(jnp.float32)
    block_count = latent_block.shape[0]
    latent_wide = latent_block.reshape(
        block_count * latent_block.shape[1], latent_block.shape[2]
    ).astype(jnp.float32)
    atom_energy, backward = jax.vjp(
        lambda feat_in, latent_in: latent_energy(feat_in, latent_in, species_codes, weights),
        features,
        latent_wide,
    )
    feature_grad, latent_grad = backward(jnp.ones_like(atom_energy))
    return (
        atom_energy.astype(jnp.bfloat16),
        feature_grad.astype(jnp.bfloat16),
        latent_grad.reshape(latent_block.shape).astype(jnp.bfloat16),
    )


def force_pull(feature_back, feature_grad_low, is_valid):
    grad_wide = lax.optimization_barrier(feature_grad_low).astype(jnp.float32)
    return feature_back(grad_wide)[0] * is_valid[None, :]


def routing(targets, peer_count, work_slots):
    slot_count = targets.shape[0]
    capacity = slot_count // peer_count
    is_live = targets >= 0
    peer_of = jnp.where(is_live, targets // work_slots, -1)
    slot_order = jnp.arange(slot_count, dtype=jnp.int32)
    same_peer = (
        (peer_of[:, None] == peer_of[None, :])
        & is_live[None, :]
        & (slot_order[None, :] < slot_order[:, None])
    )
    rank_in = jnp.sum(same_peer.astype(jnp.int32), axis=1)
    position = jnp.where(is_live, peer_of * capacity + rank_in, 0)
    pick_table = is_live[:, None] & (position[:, None] == slot_order[None, :])
    source = jnp.sum(pick_table.astype(jnp.int32) * slot_order[:, None], axis=0)
    filled = jnp.any(pick_table, axis=0)
    slot_marks = jnp.where(filled, jnp.take(targets % work_slots, source), -1)
    return (source, filled, slot_marks, position, is_live)


def row_mask(flags, values):
    return flags.reshape((-1,) + (1,) * (values.ndim - 1)).astype(values.dtype)


def pack_rows(values, source, filled):
    picked = jnp.take(values, source, axis=0)
    return picked * row_mask(filled, picked)


def settle_rows(values, slot_marks, work_slots):
    slot_order = jnp.arange(slot_marks.shape[0], dtype=jnp.int32)
    wanted = jnp.arange(work_slots, dtype=jnp.int32)
    source = jnp.sum(
        (slot_marks[None, :] == wanted[:, None]).astype(jnp.int32) * slot_order[None, :], axis=1
    )
    return jnp.take(values, source, axis=0)


def answer_rows(values, slot_marks):
    picked = jnp.take(values, jnp.maximum(slot_marks, 0), axis=0)
    return picked * row_mask(slot_marks >= 0, picked)


def unpack_rows(values, position, is_live):
    picked = jnp.take(values, position, axis=0)
    return picked * row_mask(is_live, picked)


def per_device(
    positions,
    species,
    neighbors,
    migration,
    latents,
    w_latent,
    w_tensor,
    w_radial,
    species_center,
    species_neighbor,
    w_hidden,
    w_update,
    w_out,
):
    weights = (
        w_latent,
        w_tensor,
        w_radial,
        species_center,
        species_neighbor,
        w_hidden,
        w_update,
        w_out,
    )
    atom_count = positions.shape[-1]
    slot_count = migration.shape[-1]
    block_edges = neighbors.shape[-1]
    work_slots = slot_count // 2
    peer_count = lax.axis_size("gx")
    own_table = jnp.concatenate(
        [positions[0, 0, 0], species[0, 0, 0][None, :].astype(jnp.float32)], axis=0
    )
    gathered = with_halo(own_table[None, None, None], (("gx", 0), ("gy", 1), ("gz", 2)), 1)
    flat_table = gathered.transpose(3, 0, 1, 2, 4).reshape(4, 27 * atom_count)
    entries = neighbors[0, 0, 0].reshape(-1)
    is_valid = entries >= 0
    safe_entry = jnp.where(is_valid, entries, 0)
    others = jnp.take(flat_table, safe_entry, axis=1)
    centers = jnp.repeat(own_table, K, axis=1)
    safe_vec = jnp.array([2.0 * cutoff_radius, 0.0, 0.0], dtype=jnp.float32)
    vectors = jnp.where(is_valid[None, :], others[:3] - centers[:3], safe_vec[:, None])
    species_codes = jnp.stack([centers[3], jnp.where(is_valid, others[3], 0.0)])
    features, feature_back = jax.vjp(edge_features, vectors)
    feature_low = features.astype(jnp.bfloat16)
    feature_rows = feature_low.shape[0]
    source, filled, slot_marks, position, is_live = routing(
        migration[0, 0, 0], peer_count, work_slots
    )
    feature_slots = feature_low.reshape(feature_rows, slot_count, block_edges).transpose(1, 0, 2)
    code_slots = (
        species_codes.reshape(2, slot_count, block_edges).transpose(1, 0, 2).astype(jnp.bfloat16)
    )
    received = (
        lax.all_to_all(
            pack_rows(latents[0, 0, 0], source, filled),
            "gx",
            split_axis=0,
            concat_axis=0,
            tiled=True,
        ),
        lax.all_to_all(
            pack_rows(feature_slots, source, filled), "gx", split_axis=0, concat_axis=0, tiled=True
        ),
        lax.all_to_all(
            pack_rows(code_slots, source, filled), "gx", split_axis=0, concat_axis=0, tiled=True
        ),
        lax.all_to_all(
            slot_marks.astype(jnp.bfloat16), "gx", split_axis=0, concat_axis=0, tiled=True
        ),
    )
    arrived_marks = received[3].astype(jnp.int32)
    work_latent = settle_rows(received[0], arrived_marks, work_slots)
    work_feature = settle_rows(received[1], arrived_marks, work_slots).transpose(1, 0, 2)
    work_feature = work_feature.reshape(feature_rows, work_slots * block_edges)
    work_codes = settle_rows(received[2], arrived_marks, work_slots).transpose(1, 0, 2)
    work_codes = work_codes.reshape(2, work_slots * block_edges).astype(jnp.float32)
    work_energy, work_grad, work_latent_grad = run_blocks(
        work_feature, work_codes, work_latent, weights
    )
    grad_slots = work_grad.reshape(feature_rows, work_slots, block_edges).transpose(1, 0, 2)
    returned = (
        lax.all_to_all(
            answer_rows(work_latent_grad, arrived_marks),
            "gx",
            split_axis=0,
            concat_axis=0,
            tiled=True,
        ),
        lax.all_to_all(
            answer_rows(grad_slots, arrived_marks), "gx", split_axis=0, concat_axis=0, tiled=True
        ),
        lax.all_to_all(
            answer_rows(work_energy.reshape(work_slots, CB), arrived_marks),
            "gx",
            split_axis=0,
            concat_axis=0,
            tiled=True,
        ),
    )
    latent_grad = unpack_rows(returned[0], position, is_live)
    grad_low = unpack_rows(returned[1], position, is_live).transpose(1, 0, 2)
    grad_low = grad_low.reshape(feature_rows, slot_count * block_edges)
    energy_low = unpack_rows(returned[2], position, is_live).reshape(atom_count)
    edge_grad = force_pull(feature_back, grad_low, is_valid.astype(jnp.float32))
    center_part = edge_grad.reshape(3, atom_count, K).sum(axis=2)
    region_part = jax.ops.segment_sum(-edge_grad.T, safe_entry, num_segments=27 * atom_count).T
    region_part = region_part.reshape(3, 27, atom_count).at[:, 13].add(center_part)
    partial_value = region_part.transpose(1, 0, 2).reshape(3, 3, 3, 3, atom_count)
    padded = with_halo(
        partial_value.astype(jnp.bfloat16), (("gx", 0), ("gy", 1), ("gz", 2)), 1
    ).astype(partial_value.dtype)
    home_force = padded[0::2, 0::2, 0::2].sum(axis=(0, 1, 2))
    force_slots = home_force.reshape(3, slot_count, CB).transpose(1, 0, 2)
    arrived = (
        lax.all_to_all(
            pack_rows(force_slots, source, filled), "gx", split_axis=0, concat_axis=0, tiled=True
        ),
        lax.all_to_all(
            slot_marks.astype(jnp.float32), "gx", split_axis=0, concat_axis=0, tiled=True
        ),
    )
    work_force = settle_rows(arrived[0], arrived[1].astype(jnp.int32), work_slots)
    forces = work_force.transpose(1, 0, 2).reshape(1, 1, 1, 3, work_slots * CB)
    return (forces, energy_low.reshape(1, 1, 1, atom_count), latent_grad[None, None, None])


def solution(mesh):
    return jax.shard_map(
        per_device,
        mesh=mesh,
        in_specs=(
            P(("parts", "gx"), "gy", "gz", None, None),
            P(("parts", "gx"), "gy", "gz", None),
            P(("parts", "gx"), "gy", "gz", None, None),
            P(("parts", "gx"), "gy", "gz", None),
            P(("parts", "gx"), "gy", "gz", None, None, None),
            P(),
            P(),
            P(),
            P(),
            P(),
            P(),
            P(),
            P(),
        ),
        out_specs=(
            P(("parts", "gx"), "gy", "gz", None, None),
            P(("parts", "gx"), "gy", "gz", None),
            P(("parts", "gx"), "gy", "gz", None, None, None),
        ),
        check_vma=False,
    )
```

profile of v0, /device:TPU:0, one launch (start us, length us, event | category | flops | bytes accessed | tf_op | source)
XLA Modules:
  0.0 570.3 jit_solution(17168355127236584620)
XLA Ops:
  3.4 5.6 collective-permute-start
  14.4 4.3 all-to-all-start.1
  25.0 4.5 collective-permute-start.2
  36.6 5.0 gather_fusion.12
  44.0 30.0 %gather_fusion.1 = f32[8192,4]{1,0:T(8,128)} fusion(f32[4,6912]{0,1:T(8,128)} %bitcast.231, s32[8192]{0:T(1024)S(1)} %broadcast_clamp_fusion), kind=kCustom, calls=%fused_computation.5 | custom fusion | bytes 294912 | tf_op jit(solution)/shard_map/jit(_take)/gather | solution.py:230
  83.0 5.1 all-to-all-start.4
  89.0 4.7 all-to-all-done.4
  93.7 3.5 all-to-all-start.3
  97.2 4.7 select_multiply_fusion.1
  101.9 5.4 all-to-all-done.3
  107.2 4.9 all-to-all-start.2
  119.7 83.0 %all-to-all-done.2 = bf16[32,256,256]{2,1,0:T(8,128)(2,1)} async-done(((bf16[32,256,256]{2,1,0:T(8,128)(2,1)}), bf16[32,256,256]{2,1,0:T(8,128)(2,1)}, u32[]{:S(2)}, u32[]{:S(2)}) %all-to-all-start.2) | async-done | bytes 4194336 | tf_op jit(solution)/shard_map/all_to_all | solution.py:246
  202.7 4.2 gather_fusion.2
  206.9 3.1 copy.487
  218.5 3.4 fusion.50
  226.3 3.2 copy.434
  229.5 3.2 copy.438
  232.6 3.2 copy.436
  250.4 3.5 fusion.33
  253.9 7.3 %fusion.22 = f32[4096,256]{0,1:T(8,128)} fusion(f32[4096,256]{0,1:T(8,128)} %copy-done.13, bf16[256,256]{1,0:T(8,128)(2,1)} %param.30, f32[4096,256]{0,1:T(8,128)} %fusion.33, bf16[256,256]{1,0:T(8,128)(2,1)} %param.31, f32[256]{0:T(256)} %convert.90, f32[4096]{0:T(1024)S(1)} %bitcast.254), kind=kOutput, calls=%fused_computation.46 | convolution fusion | flops 1101004800 | bytes 12862464 | tf_op jit(solution)/shard_map/transpose(jvp())/dot_general | solution.py:108
  261.2 6.6 %fusion.26 = (f32[4096]{0:T(1024)}, f32[4096,256]{0,1:T(8,128)}) fusion(f32[256]{0:T(256)} %convert.90, f32[4096]{0:T(1024)S(1)} %bitcast.255, bf16[256,256]{1,0:T(8,128)(2,1)} %param.31, f32[4096,256]{0,1:T(8,128)} %fusion.33), kind=kOutput, calls=%fused_computation.48 | convolution fusion | flops 547352576 | bytes 8553472 | tf_op jit(solution)/shard_map/jvp()/dot_general | solution.py:112
  272.6 3.5 slice_multiply_fusion.2
  276.1 3.3 copy.450
  279.4 3.7 fusion.53
  283.1 4.2 fusion.48
  287.3 3.3 copy.452
  290.5 3.3 convolution_bitcast_fusion.2
  293.8 5.7 %convolution_bitcast_fusion.1 = f32[128,32,1]{1,2,0:T(1,128)} fusion(f32[128,32,64]{2,1,0:T(8,128)} %bitcast.220, f32[128,64,9]{1,2,0:T(8,128)S(1)} %convolution_multiply_fusion), kind=kOutput, calls=%fused_computation.78 | convolution fusion | flops 3145728 | bytes 1130496 | tf_op jit(solution)/shard_map/transpose(jvp(akm,acm->akc))/dot_general | solution.py:91
  299.5 3.3 copy.451
  302.8 5.1 fusion.56
  310.0 3.1 fusion.45
  313.1 3.7 convolution_add_fusion.4
  327.5 3.7 all-to-all-start.5
  331.3 11.1 %all-to-all-done.5 = bf16[32,18,256]{2,1,0:T(8,128)(2,1)S(1)} async-done(((bf16[32,18,256]{2,1,0:T(8,128)(2,1)}), bf16[32,18,256]{2,1,0:T(8,128)(2,1)S(1)}, u32[]{:S(2)}, u32[]{:S(2)}) %all-to-all-start.5) | async-done | bytes 294944 | tf_op jit(solution)/shard_map/all_to_all | solution.py:281
  342.3 3.2 all-to-all-start
  352.3 55.6 %scatter_custom_fusion = f32[6912,3]{1,0:T(8,128)} fusion(s32[8192]{0:T(1024)} %bitcast.297, f32[8192,3]{1,0:T(8,128)} %copy.458, f32[]{:T(128)} %constant.267.clone.1), kind=kCustom, calls=%fused_computation.69 | custom fusion | flops 24576 | bytes 83456 | tf_op jit(solution)/shard_map/scatter-add | solution.py:298
  414.0 4.5 collective-permute-start.6
  420.1 4.6 collective-permute-start.8
  426.0 5.4 fusion.14
  435.8 3.3 copy.491
  443.5 5.0 all-to-all-start.7
  449.4 4.8 all-to-all-done.7
  454.1 3.2 all-to-all-start.6
  457.3 4.7 select_multiply_fusion.2
  462.9 4.9 all-to-all-start.8
  472.1 88.3 %all-to-all-done.8 = bf16[32,256,256]{2,1,0:T(8,128)(2,1)} async-done(((bf16[32,256,256]{2,1,0:T(8,128)(2,1)}), bf16[32,256,256]{2,1,0:T(8,128)(2,1)}, u32[]{:S(2)}, u32[]{:S(2)}) %all-to-all-start.8) | async-done | bytes 4194336 | tf_op jit(solution)/shard_map/all_to_all | solution.py:274
  560.4 5.0 gather_fusion.15
  565.4 4.6 fusion.27
  (338 shorter events, 115.8 us)
Async XLA Ops:
  0.6 209.3 %copy-start = (bf16[256,384]{1,0:T(8,128)(2,1)S(1)}, bf16[256,384]{1,0:T(8,128)(2,1)}, u32[]{:S(2)}) copy-start(bf16[256,384]{1,0:T(8,128)(2,1)} %param.25) | copy-start | bytes 589828
  2.1 21.6 %collective-permute-start.1 = (f32[1,1,1,4,256]{4,3,2,1,0:T(4,128)S(1)}, f32[1,1,1,4,256]{4,3,2,1,0:T(4,128)S(1)}, u32[]{:S(2)}, u32[]{:S(2)}) collective-permute-start(f32[1,1,1,4,256]{4,3,2,1,0:T(4,128)S(1)} %maximum_bitcast_fusion.2), channel_id=1, source_target_pairs={{4,0},{8,4},{12,8},{5,1},{9,5},{13,9},{6,2},{10,6},{14,10},{7,3},{... | collective-permute-start | bytes 12296 | tf_op jit(solution)/shard_map/ppermute | solution.py:27
  3.4 20.3 %collective-permute-start = (f32[1,1,1,4,256]{4,3,2,1,0:T(4,128)S(1)}, f32[1,1,1,4,256]{4,3,2,1,0:T(4,128)S(1)}, u32[]{:S(2)}, u32[]{:S(2)}) collective-permute-start(f32[1,1,1,4,256]{4,3,2,1,0:T(4,128)S(1)} %maximum_bitcast_fusion.2), channel_id=1, source_target_pairs={{0,4},{4,8},{8,12},{1,5},{5,9},{9,13},{2,6},{6,10},{10,14},{3,7},{... | collective-permute-start | bytes 12296 | tf_op jit(solution)/shard_map/ppermute | solution.py:25
  12.4 64.6 %copy-start.52 = (s32[1024]{0:T(1024)}, s32[1024]{0:T(1024)S(1)}, u32[]{:S(2)}) copy-start(s32[1024]{0:T(1024)S(1)} %pad_clamp_fusion.6) | copy-start | bytes 12292
  14.4 68.5 %all-to-all-start.1 = ((bf16[4,8,1]{1,2,0:T(2,128)(2,1)}), bf16[4,8,1]{1,2,0:T(2,128)(2,1)S(1)}, u32[]{:S(2)}, u32[]{:S(2)}) async-start(bf16[4,8,1]{1,2,0:T(2,128)(2,1)} %copy.417), calls=%async_computation.1 | async-start | bytes 4096 | tf_op jit(solution)/shard_map/all_to_all | solution.py:259
  19.3 77.9 %copy-start.46 = (pred[32]{0:T(512)(128)(4,1)}, pred[32]{0:T(512)(128)(4,1)S(1)}, u32[]{:S(2)}) copy-start(pred[32]{0:T(512)(128)(4,1)S(1)} %get-tuple-element.117) | copy-start | bytes 100
  23.7 5.9 %collective-permute-start.3 = (f32[3,1,1,4,256]{4,3,2,1,0:T(4,128)S(1)}, f32[3,1,1,4,256]{4,3,2,1,0:T(4,128)S(1)}, u32[]{:S(2)}, u32[]{:S(2)}) collective-permute-start(f32[3,1,1,4,256]{4,3,2,1,0:T(4,128)S(1)} %pad_maximum_fusion.10), channel_id=1, source_target_pairs={{2,0},{3,1},{6,4},{7,5},{10,8},{11,9},{14,12},{15,13},{18,16},{19,... | collective-permute-start | bytes 36872 | tf_op jit(solution)/shard_map/ppermute | solution.py:27
  25.0 5.9 %collective-permute-start.2 = (f32[3,1,1,4,256]{4,3,2,1,0:T(4,128)S(1)}, f32[3,1,1,4,256]{4,3,2,1,0:T(4,128)S(1)}, u32[]{:S(2)}, u32[]{:S(2)}) collective-permute-start(f32[3,1,1,4,256]{4,3,2,1,0:T(4,128)S(1)} %pad_maximum_fusion.10), channel_id=1, source_target_pairs={{0,2},{1,3},{4,6},{5,7},{8,10},{9,11},{12,14},{13,15},{16,18},{17,... | collective-permute-start | bytes 36872 | tf_op jit(solution)/shard_map/ppermute | solution.py:25
  30.9 10.6 %collective-permute-start.5 = (f32[3,3,1,4,256]{4,3,2,1,0:T(4,128)S(1)}, f32[3,3,1,4,256]{4,3,2,1,0:T(4,128)S(1)}, u32[]{:S(2)}, u32[]{:S(2)}) collective-permute-start(f32[3,3,1,4,256]{4,3,2,1,0:T(4,128)S(1)} %pad_maximum_fusion.6), channel_id=1, source_target_pairs={{1,0},{3,2},{5,4},{7,6},{9,8},{11,10},{13,12},{15,14},{17,16},{19,... | collective-permute-start | bytes 110600 | tf_op jit(solution)/shard_map/ppermute | solution.py:27
  32.2 9.4 %collective-permute-start.4 = (f32[3,3,1,4,256]{4,3,2,1,0:T(4,128)S(1)}, f32[3,3,1,4,256]{4,3,2,1,0:T(4,128)S(1)}, u32[]{:S(2)}, u32[]{:S(2)}) collective-permute-start(f32[3,3,1,4,256]{4,3,2,1,0:T(4,128)S(1)} %pad_maximum_fusion.6), channel_id=1, source_target_pairs={{0,1},{2,3},{4,5},{6,7},{8,9},{10,11},{12,13},{14,15},{16,17},{18,... | collective-permute-start | bytes 110600 | tf_op jit(solution)/shard_map/ppermute | solution.py:25
  35.9 44.6 %copy-start.55 = (f32[8]{0:T(128)}, f32[8]{0:T(128)S(1)}, u32[]{:S(2)}) copy-start(f32[8]{0:T(128)S(1)} %get-tuple-element.119) | copy-start | bytes 100
  41.6 36.1 %copy-start.62 = (f32[3]{0:T(128)S(1)}, f32[3]{0:T(128)}, u32[]{:S(2)}) copy-start(f32[3]{0:T(128)} %constant.289.clone) | copy-start | bytes 40
  83.0 30.9 %copy-start.43 = (bf16[4,8,1]{1,2,0:T(2,128)(2,1)}, bf16[4,8,1]{1,2,0:T(2,128)(2,1)S(1)}, u32[]{:S(2)}) copy-start(bf16[4,8,1]{1,2,0:T(2,128)(2,1)S(1)} %all-to-all-done.1) | copy-start | bytes 196
  83.0 10.8 %all-to-all-start.4 = ((bf16[32,2,256]{2,1,0:T(2,128)(2,1)}), bf16[32,2,256]{2,1,0:T(2,128)(2,1)S(1)}, u32[]{:S(2)}, u32[]{:S(2)}) async-start(bf16[32,2,256]{2,1,0:T(2,128)(2,1)} %fusion.97), calls=%async_computation.4 | async-start | bytes 65536 | tf_op jit(solution)/shard_map/all_to_all | solution.py:256
  93.7 13.5 %all-to-all-start.3 = ((bf16[32,18,256]{2,1,0:T(8,128)(2,1)}), bf16[32,18,256]{2,1,0:T(8,128)(2,1)S(1)}, u32[]{:S(2)}, u32[]{:S(2)}) async-start(bf16[32,18,256]{2,1,0:T(8,128)(2,1)} %select_multiply_fusion.4), calls=%async_computation.3 | async-start | bytes 786432 | tf_op jit(solution)/shard_map/all_to_all | solution.py:253
  101.9 10.3 %copy-start.67 = (bf16[256]{0:T(256)(128)(2,1)S(1)}, bf16[256]{0:T(256)(128)(2,1)}, u32[]{:S(2)}) copy-start(bf16[256]{0:T(256)(128)(2,1)} %param.32) | copy-start | bytes 1540
  107.2 95.4 %all-to-all-start.2 = ((bf16[32,256,256]{2,1,0:T(8,128)(2,1)}), bf16[32,256,256]{2,1,0:T(8,128)(2,1)}, u32[]{:S(2)}, u32[]{:S(2)}) async-start(bf16[32,256,256]{2,1,0:T(8,128)(2,1)} %select_multiply_fusion.1), calls=%async_computation.2 | async-start | bytes 8388608 | tf_op jit(solution)/shard_map/all_to_all | solution.py:246
  114.2 95.8 %copy-start.40 = (pred[4096]{0:T(1024)(128)(4,1)}, pred[4096]{0:T(1024)(128)(4,1)S(1)}, u32[]{:S(2)}) copy-start(pred[4096]{0:T(1024)(128)(4,1)S(1)} %broadcast_in_dim.234) | copy-start | bytes 12292
  117.5 89.3 %copy-start.16 = (bf16[3,8,16,256]{3,1,2,0:T(8,128)(2,1)}, bf16[3,8,16,256]{3,1,2,0:T(8,128)(2,1)S(1)}, u32[]{:S(2)}) copy-start(bf16[3,8,16,256]{3,1,2,0:T(8,128)(2,1)S(1)} %copy.497) | copy-start | bytes 589828
  117.8 89.1 %copy-start.6 = (bf16[128,32,9]{1,0,2:T(8,128)(2,1)}, bf16[128,32,9]{1,0,2:T(8,128)(2,1)S(1)}, u32[]{:S(2)}) copy-start(bf16[128,32,9]{1,0,2:T(8,128)(2,1)S(1)} %reshape.827) | copy-start | bytes 221188
  302.8 10.3 %copy-start.3 = (f32[4096,64]{1,0:T(8,128)S(1)}, f32[4096,64]{1,0:T(8,128)}, u32[]{:S(2)}) copy-start(f32[4096,64]{1,0:T(8,128)} %copy.432) | copy-start | bytes 3145732
  302.8 10.3 %copy-start.14 = (f32[128,32,5]{1,2,0:T(8,128)S(1)}, f32[128,32,5]{1,2,0:T(8,128)}, u32[]{:S(2)}) copy-start(f32[128,32,5]{1,2,0:T(8,128)} %fusion.48) | copy-start | bytes 245764
  322.6 23.5 %copy-start.50 = (pred[32]{0:T(512)(128)(4,1)S(1)}, pred[32]{0:T(512)(128)(4,1)}, u32[]{:S(2)}) copy-start(pred[32]{0:T(512)(128)(4,1)} %get-tuple-element.45) | copy-start | bytes 100
  322.6 23.5 %copy-start.51 = (bf16[32]{0:T(256)(128)(2,1)S(1)}, bf16[32]{0:T(256)(128)(2,1)}, u32[]{:S(2)}) copy-start(bf16[32]{0:T(256)(128)(2,1)} %get-tuple-element.110) | copy-start | bytes 196
  325.7 21.1 %copy-start.20 = (f32[1,8192]{1,0:T(1,128)S(1)}, f32[1,8192]{1,0:T(1,128)}, u32[]{:S(2)}) copy-start(f32[1,8192]{1,0:T(1,128)} %copy-done.19) | copy-start | bytes 98308
  325.7 21.1 %copy-start.26 = (f32[1,8192]{1,0:T(1,128)S(1)}, f32[1,8192]{1,0:T(1,128)}, u32[]{:S(2)}) copy-start(f32[1,8192]{1,0:T(1,128)} %copy-done.25) | copy-start | bytes 98308
  325.7 21.1 %copy-start.30 = (f32[1,8192]{1,0:T(1,128)S(1)}, f32[1,8192]{1,0:T(1,128)}, u32[]{:S(2)}) copy-start(f32[1,8192]{1,0:T(1,128)} %copy-done.29) | copy-start | bytes 98308
  325.8 21.6 %copy-start.24 = (f32[8192]{0:T(1024)S(1)}, f32[8192]{0:T(1024)}, u32[]{:S(2)}) copy-start(f32[8192]{0:T(1024)} %copy-done.23) | copy-start | bytes 98308
  325.8 21.6 %copy-start.33 = (f32[8192]{0:T(1024)S(1)}, f32[8192]{0:T(1024)}, u32[]{:S(2)}) copy-start(f32[8192]{0:T(1024)} %get-tuple-element.91) | copy-start | bytes 98308
  325.8 21.6 %copy-start.56 = (f32[8]{0:T(128)S(1)}, f32[8]{0:T(128)}, u32[]{:S(2)}) copy-start(f32[8]{0:T(128)} %copy-done.55) | copy-start | bytes 100
  325.9 21.6 %copy-start.61 = (f32[8]{0:T(128)S(1)}, f32[8]{0:T(128)}, u32[]{:S(2)}) copy-start(f32[8]{0:T(128)} %get-tuple-element.118) | copy-start | bytes 100
  326.6 22.5 %copy-start.28 = (f32[8192]{0:T(1024)S(1)}, f32[8192]{0:T(1024)}, u32[]{:S(2)}) copy-start(f32[8192]{0:T(1024)} %copy-done.27) | copy-start | bytes 98308
  326.6 22.5 %copy-start.35 = (f32[1,8192]{1,0:T(1,128)S(1)}, f32[1,8192]{1,0:T(1,128)}, u32[]{:S(2)}) copy-start(f32[1,8192]{1,0:T(1,128)} %get-tuple-element.83) | copy-start | bytes 98308
  326.6 22.5 %copy-start.36 = (f32[1,8192]{1,0:T(1,128)S(1)}, f32[1,8192]{1,0:T(1,128)}, u32[]{:S(2)}) copy-start(f32[1,8192]{1,0:T(1,128)} %get-tuple-element.84) | copy-start | bytes 98308
  326.6 22.5 %copy-start.37 = (f32[1,8192]{1,0:T(1,128)S(1)}, f32[1,8192]{1,0:T(1,128)}, u32[]{:S(2)}) copy-start(f32[1,8192]{1,0:T(1,128)} %get-tuple-element.88) | copy-start | bytes 98308
  326.6 22.6 %copy-start.34 = (f32[8192]{0:T(1024)S(1)}, f32[8192]{0:T(1024)}, u32[]{:S(2)}) copy-start(f32[8192]{0:T(1024)} %get-tuple-element.43) | copy-start | bytes 98308
  327.5 14.8 %all-to-all-start.5 = ((bf16[32,18,256]{2,1,0:T(8,128)(2,1)}), bf16[32,18,256]{2,1,0:T(8,128)(2,1)S(1)}, u32[]{:S(2)}, u32[]{:S(2)}) async-start(bf16[32,18,256]{2,1,0:T(8,128)(2,1)} %select_multiply_fusion.5), calls=%async_computation.5 | async-start | bytes 786432 | tf_op jit(solution)/shard_map/all_to_all | solution.py:281
  342.3 101.2 %all-to-all-start = ((f32[4,8,1]{1,2,0:T(1,128)}), f32[4,8,1]{1,2,0:T(1,128)S(1)}, u32[]{:S(2)}, u32[]{:S(2)}) async-start(f32[4,8,1]{1,2,0:T(1,128)} %bitcast.3), calls=%async_computation | async-start | bytes 4096 | tf_op jit(solution)/shard_map/all_to_all | solution.py:310
  409.7 16.2 %copy-start.68 = (f32[256]{0:T(256)S(1)}, f32[256]{0:T(256)}, u32[]{:S(2)}) copy-start(f32[256]{0:T(256)} %convert.90) | copy-start | bytes 3076
  412.7 6.7 %collective-permute-start.7 = (bf16[1,3,3,3,256]{4,3,2,1,0:T(4,128)(2,1)S(1)}, bf16[1,3,3,3,256]{4,3,2,1,0:T(4,128)(2,1)S(1)}, u32[]{:S(2)}, u32[]{:S(2)}) collective-permute-start(bf16[1,3,3,3,256]{4,3,2,1,0:T(4,128)(2,1)S(1)} %bitcast.299), channel_id=1, source_target_pairs={{4,0},{8,4},{12,8},{5,1},{9,5},{13,9},{6,2},{10,6},{14,10},{7,3},{... | collective-permute-start | bytes 41480 | tf_op jit(solution)/shard_map/ppermute | solution.py:27
  414.0 6.0 %collective-permute-start.6 = (bf16[1,3,3,3,256]{4,3,2,1,0:T(4,128)(2,1)S(1)}, bf16[1,3,3,3,256]{4,3,2,1,0:T(4,128)(2,1)S(1)}, u32[]{:S(2)}, u32[]{:S(2)}) collective-permute-start(bf16[1,3,3,3,256]{4,3,2,1,0:T(4,128)(2,1)S(1)} %bitcast.298), channel_id=1, source_target_pairs={{0,4},{4,8},{8,12},{1,5},{5,9},{9,13},{2,6},{6,10},{10,14},{3,7},{... | collective-permute-start | bytes 41480 | tf_op jit(solution)/shard_map/ppermute | solution.py:25
  420.1 12.4 %collective-permute-start.8 = (bf16[5,1,3,3,256]{4,3,2,1,0:T(4,128)(2,1)S(1)}, bf16[5,1,3,3,256]{4,3,2,1,0:T(4,128)(2,1)S(1)}, u32[]{:S(2)}, u32[]{:S(2)}) collective-permute-start(bf16[5,1,3,3,256]{4,3,2,1,0:T(4,128)(2,1)S(1)} %get-tuple-element.89), channel_id=1, source_target_pairs={{0,2},{1,3},{4,6},{5,7},{8,10},{9,11},{12,14},{13,15},{16,18},{17,... | collective-permute-start | bytes 69128 | tf_op jit(solution)/shard_map/ppermute | solution.py:25
  424.7 7.8 %collective-permute-start.9 = (bf16[5,1,3,3,256]{4,3,2,1,0:T(4,128)(2,1)S(1)}, bf16[5,1,3,3,256]{4,3,2,1,0:T(4,128)(2,1)S(1)}, u32[]{:S(2)}, u32[]{:S(2)}) collective-permute-start(bf16[5,1,3,3,256]{4,3,2,1,0:T(4,128)(2,1)S(1)} %get-tuple-element.90), channel_id=1, source_target_pairs={{2,0},{3,1},{6,4},{7,5},{10,8},{11,9},{14,12},{15,13},{18,16},{19,... | collective-permute-start | bytes 69128 | tf_op jit(solution)/shard_map/ppermute | solution.py:27
  432.6 9.5 %collective-permute-start.10 = (bf16[5,5,1,3,256]{4,3,2,1,0:T(4,128)(2,1)S(1)}, bf16[5,5,1,3,256]{4,3,2,1,0:T(4,128)(2,1)S(1)}, u32[]{:S(2)}, u32[]{:S(2)}) collective-permute-start(bf16[5,5,1,3,256]{4,3,2,1,0:T(4,128)(2,1)S(1)} %get-tuple-element.81), channel_id=1, source_target_pairs={{0,1},{2,3},{4,5},{6,7},{8,9},{10,11},{12,13},{14,15},{16,17},{18,... | collective-permute-start | bytes 115208 | tf_op jit(solution)/shard_map/ppermute | solution.py:25
  433.9 8.2 %collective-permute-start.11 = (bf16[5,5,1,3,256]{4,3,2,1,0:T(4,128)(2,1)S(1)}, bf16[5,5,1,3,256]{4,3,2,1,0:T(4,128)(2,1)S(1)}, u32[]{:S(2)}, u32[]{:S(2)}) collective-permute-start(bf16[5,5,1,3,256]{4,3,2,1,0:T(4,128)(2,1)S(1)} %get-tuple-element.82), channel_id=1, source_target_pairs={{1,0},{3,2},{5,4},{7,6},{9,8},{11,10},{13,12},{15,14},{17,16},{19,... | collective-permute-start | bytes 115208 | tf_op jit(solution)/shard_map/ppermute | solution.py:27
  443.5 10.6 %all-to-all-start.7 = ((bf16[4,8,8]{2,1,0:T(8,128)(2,1)}), bf16[4,8,8]{2,1,0:T(8,128)(2,1)S(1)}, u32[]{:S(2)}, u32[]{:S(2)}) async-start(bf16[4,8,8]{2,1,0:T(8,128)(2,1)} %fusion.103), calls=%async_computation.7 | async-start | bytes 16384 | tf_op jit(solution)/shard_map/all_to_all | solution.py:284
  454.1 8.7 %all-to-all-start.6 = ((f32[4,1,192]{2,1,0:T(1,128)}), f32[4,1,192]{2,1,0:T(1,128)S(1)}, u32[]{:S(2)}, u32[]{:S(2)}) async-start(f32[4,1,192]{2,1,0:T(1,128)} %reshape.1019), calls=%async_computation.6 | async-start | bytes 8192 | tf_op jit(solution)/shard_map/all_to_all | solution.py:307
  462.9 97.5 %all-to-all-start.8 = ((bf16[32,256,256]{2,1,0:T(8,128)(2,1)}), bf16[32,256,256]{2,1,0:T(8,128)(2,1)}, u32[]{:S(2)}, u32[]{:S(2)}) async-start(bf16[32,256,256]{2,1,0:T(8,128)(2,1)} %select_multiply_fusion.2), calls=%async_computation.8 | async-start | bytes 8388608 | tf_op jit(solution)/shard_map/all_to_all | solution.py:274
  (42 other events, 188.9 us)
where the time goes:
time: 579 us; the launch traced here: 570 us
  waiting for transfers between devices  200 us (35%)
  local copies, waits for them, and re-layouts  115 us (20%)
  other arithmetic  104 us (18%)
  matrix products  79.8 us (14%)
  starting transfers between devices  69 us (12%)
    all_to_all x1, waiting for transfers between devices, per_device(): lax.all_to_all(answer_rows(work_latent_grad, arrived_marks), 'gx', split_...  88.3 us
    all_to_all x1, waiting for transfers between devices, per_device(): lax.all_to_all(pack_rows(latents[0, 0, 0], source, filled), 'gx', split_a...  83 us
    scatter-add x1, other arithmetic, per_device(): jax.ops.segment_sum(-edge_grad.T, safe_entry, num_segments=27 * atom_count)  55.6 us
    gather x2, local copies, waits for them, and re-layouts, per_device(): others = jnp.take(flat_table, safe_entry, axis=1)  32.8 us
    dot_general x8, matrix products, latent_energy(): jnp.einsum('akm,acm->akc', harm_atoms[:, :, first_m:last_m], environment[...  29.9 us
    ppermute x6, starting transfers between devices, with_halo(): lax.ppermute(tail, axis, [(i, (i + 1) % count) for i in range(ends)])  23.6 us
  transfers between devices with their start and end apart: 21, of which 9 were waited for; matrix products, arithmetic and copies ran while one was open for 29% of the time, Pallas kernels for 0%

commit v1 on v0

v1 whole, which is shorter than its diff:
```python
import functools

import jax
import jax.numpy as jnp
import numpy as np
from jax import lax
from jax.experimental import pallas as pl
from jax.experimental.pallas import tpu as pltpu
from jax.sharding import PartitionSpec as P

NB = 8
CB = 8
K = 32
FR = 32
TILE_BLOCKS = 2

cutoff_radius = 6.0
sqrt_three = 3.0**0.5
sqrt_five = 5.0**0.5
sqrt_fifteen = 15.0**0.5
radial_scale = (2.0 / cutoff_radius) ** 0.5
f32 = jnp.float32
bf16 = jnp.bfloat16

COLUMNS = ((0, 1), (-1, 2), (-1, 3), (4, 5), (6, 7), (8, -1))


def with_halo(cells, sides, width):
    for axis, dim in sides:
        count = lax.axis_size(axis)
        ends = count - 1
        head = lax.slice_in_dim(cells, 0, width, axis=dim)
        tail = lax.slice_in_dim(cells, cells.shape[dim] - width, cells.shape[dim], axis=dim)
        cells = jnp.concatenate(
            [
                lax.ppermute(tail, axis, [(i, (i + 1) % count) for i in range(ends)]),
                cells,
                lax.ppermute(head, axis, [((i + 1) % count, i) for i in range(ends)]),
            ],
            axis=dim,
        )
    return cells


def sin_cos(angle):
    phi = angle - np.float32(np.pi / 2)
    sq = phi * phi
    cos_phi = 1.0
    coeffs = [1.0]
    for n in range(1, 8):
        coeffs.append(-coeffs[-1] / ((2 * n - 1) * (2 * n)))
    cos_phi = jnp.full_like(sq, coeffs[-1])
    for c in coeffs[-2::-1]:
        cos_phi = cos_phi * sq + c
    coeffs = [1.0]
    for n in range(1, 8):
        coeffs.append(-coeffs[-1] / ((2 * n) * (2 * n + 1)))
    sin_phi = jnp.full_like(sq, coeffs[-1])
    for c in coeffs[-2::-1]:
        sin_phi = sin_phi * sq + c
    sin_phi = sin_phi * phi
    return cos_phi, -sin_phi


def sigmoid(x):
    return 0.5 * jnp.tanh(0.5 * x) + 0.5


def dot(a, b):
    return jnp.dot(a, b, preferred_element_type=f32)


def geometry(rows, nbr_ref, own_ref, tab_ref, vec_s, feat_s):
    hs, eb = nbr_ref.shape
    lane = lax.broadcasted_iota(jnp.int32, (hs, eb), 1)
    atom = lane // K
    centers = []
    for c in range(4):
        own = own_ref[c]
        acc = jnp.broadcast_to(own[:, 0:1], (hs, eb))
        for a in range(1, CB):
            acc = jnp.where(atom == a, own[:, a : a + 1], acc)
        centers.append(acc)
    nbr = nbr_ref[...]
    valid = nbr >= 0
    safe = jnp.where(valid, nbr, 0)
    row_of = safe // 128
    lane_of = safe % 128
    halves = eb // 128

    def look(q, acc):
        out = []
        for c in range(4):
            src = jnp.broadcast_to(tab_ref[c, pl.ds(q, 1), :], (hs, 128))
            for h in range(halves):
                got = jnp.take_along_axis(
                    src, lane_of[:, h * 128 : (h + 1) * 128], axis=1, mode="promise_in_bounds"
                )
                out.append(jnp.where(row_of[:, h * 128 : (h + 1) * 128] == q, got, acc[c * halves + h]))
        return tuple(out)

    found = lax.fori_loop(
        0, rows, look, tuple(jnp.zeros((hs, 128), f32) for _ in range(4 * halves))
    )
    others = [jnp.concatenate(found[c * halves : (c + 1) * halves], axis=1) for c in range(4)]
    safe_vec = (2.0 * cutoff_radius, 0.0, 0.0)
    for c in range(3):
        vec_s[c] = jnp.where(valid, others[c] - centers[c], safe_vec[c])
    kinds_nbr = jnp.where(valid, others[3], 0.0)
    x, y, z = vec_s[0], vec_s[1], vec_s[2]
    square = x * x + y * y + z * z
    length = jnp.sqrt(square)
    inv = 1.0 / length
    ux, uy, uz = x * inv, y * inv, z * inv
    near = jnp.maximum(1.0 - square / (cutoff_radius * cutoff_radius), 0.0)
    cut = near * near
    angle = jnp.minimum(length, cutoff_radius) * np.float32(np.pi / cutoff_radius)
    sin_one, cos_one = sin_cos(angle)
    feats = [
        jnp.ones_like(x),
        sqrt_three * ux,
        sqrt_three * uy,
        sqrt_three * uz,
        sqrt_fifteen * ux * uy,
        sqrt_fifteen * uy * uz,
        0.5 * sqrt_five * (3.0 * uz * uz - 1.0),
        sqrt_fifteen * ux * uz,
        0.5 * sqrt_fifteen * (ux * ux - uy * uy),
    ]
    before, now = jnp.zeros_like(x), sin_one
    scale = radial_scale * inv * cut
    for _ in range(NB):
        feats.append(now * scale)
        before, now = now, 2.0 * cos_one * now - before
    feats.append(cut)
    for f, value in enumerate(feats):
        feat_s[:, f, :] = value.astype(bf16).astype(f32)
    base = len(feats)
    for kinds in (centers[3], kinds_nbr):
        for s in range(5):
            feat_s[:, base, :] = jnp.where(kinds == float(s), 1.0, 0.0)
            base += 1
    while base < FR:
        feat_s[:, base, :] = jnp.zeros_like(x)
        base += 1


def network(tile, lat_ref, wp, sel_y, w1, wf, wh, v2, wb, wt, wl, sel_g, wo, feat_s, grad_s, out_ref):
    first = tile * TILE_BLOCKS
    eb = lat_ref.shape[1]
    te = TILE_BLOCKS * eb
    atoms = te // K
    feat = jnp.concatenate([feat_s[first + t] for t in range(TILE_BLOCKS)], axis=1)
    feat_t = jnp.concatenate([feat, feat], axis=0).T
    env = feat_t[:, 17:18]
    feat_low = feat_t.astype(bf16)
    lat = lat_ref[...].reshape(te, lat_ref.shape[2])
    proj = dot(lat, wp[...])
    harm = dot(feat_low, sel_y[...])
    pe = proj[:, :128]
    vw = proj[:, 128:256]
    read = proj[:, 256:257]
    ew = pe * env
    norm = 1.0 / K**0.5

    def over_atom(value):
        summed = jnp.sum(value.reshape(atoms, K, 128), axis=1, keepdims=True) * norm
        return jnp.broadcast_to(summed, (atoms, K, 128)).reshape(te, 128)

    ys = [harm[:, c * 128 : (c + 1) * 128] for c in range(6)]
    envs = [over_atom(ew * yc) for yc in ys]
    ea_a = ys[0] * envs[0] + ys[1] * envs[1] + ys[2] * envs[2]
    ea_b = ys[3] * envs[3] + ys[4] * envs[4] + ys[5] * envs[5]
    inv = jnp.concatenate([(vw * ea_a).astype(bf16), (vw * ea_b).astype(bf16)], axis=1)
    p1 = dot(jnp.concatenate([lat, inv], axis=1), w1[...]) + dot(feat_low, wf[...])
    s1 = sigmoid(p1)
    h1 = p1 * s1
    d1 = s1 + h1 * (1.0 - s1)
    p2 = dot(h1.astype(bf16), wh[...])
    s2 = sigmoid(p2)
    h2 = p2 * s2
    d2 = s2 + h2 * (1.0 - s2)
    up = dot(h2.astype(bf16), v2[...])
    up = up[:, 0:1] + up[:, 1:2]
    back = dot(d2.astype(bf16), wb[...])
    g1 = ((env * env) * (d1 * back)).astype(bf16)
    gx = dot(g1, wt[...])
    gx_a, gx_b = gx[:, :128], gx[:, 128:]
    gea_a, gea_b = gx_a * vw, gx_b * vw
    gv = gx_a * ea_a + gx_b * ea_b
    gew = jnp.zeros_like(gv)
    pieces = []
    for c in range(6):
        gea = gea_a if c < 3 else gea_b
        genv = over_atom(ys[c] * gea)
        gew = gew + ys[c] * genv
        pieces.append((ew * genv + gea * envs[c]).astype(bf16))
    pieces.append(g1)
    pieces.append((pe * gew).astype(bf16))
    gf = dot(jnp.concatenate(pieces, axis=1), sel_g[...])
    lane = lax.broadcasted_iota(jnp.int32, gf.shape, 1)
    gf = gf + jnp.where(lane == 17, read + 2.0 * env * up, 0.0)
    gf = jnp.where(lane == 18, env * (read + env * up), gf)
    gft = gf.T
    for t in range(TILE_BLOCKS):
        grad_s[first + t] = gft[:, t * eb : (t + 1) * eb]
    glat = dot(
        jnp.concatenate([g1, gv.astype(bf16), (gew * env).astype(bf16)], axis=1), wl[...]
    )
    glat = glat + env * wo[...]
    out_ref[...] = glat.astype(bf16).reshape(out_ref.shape)


def pull(rows, nbr_ref, vec_s, grad_s, edge_s, part_ref, center_ref, energy_ref):
    hs, eb = nbr_ref.shape
    valid = nbr_ref[...] >= 0
    x, y, z = vec_s[0], vec_s[1], vec_s[2]
    g = [grad_s[:, f, :] for f in range(19)]
    square = x * x + y * y + z * z
    length = jnp.sqrt(square)
    inv = 1.0 / length
    ux, uy, uz = x * inv, y * inv, z * inv
    near = jnp.maximum(1.0 - square / (cutoff_radius * cutoff_radius), 0.0)
    cut = near * near
    cut_d = (-4.0 / (cutoff_radius * cutoff_radius)) * length * near
    angle = jnp.minimum(length, cutoff_radius) * np.float32(np.pi / cutoff_radius)
    sin_one, cos_one = sin_cos(angle)
    sum_sin = jnp.zeros_like(x)
    sum_cos = jnp.zeros_like(x)
    s_before, s_now = jnp.zeros_like(x), sin_one
    c_before, c_now = jnp.ones_like(x), cos_one
    for n in range(1, NB + 1):
        sum_sin = sum_sin + g[8 + n] * s_now
        sum_cos = sum_cos + (n * np.pi / cutoff_radius) * (g[8 + n] * c_now)
        s_before, s_now = s_now, 2.0 * cos_one * s_now - s_before
        c_before, c_now = c_now, 2.0 * cos_one * c_now - c_before
    along = radial_scale * inv * (cut * sum_cos + (cut_d - cut * inv) * sum_sin) + g[17] * cut_d
    gx = sqrt_three * g[1] + sqrt_fifteen * (uy * g[4] + uz * g[7] + ux * g[8])
    gy = sqrt_three * g[2] + sqrt_fifteen * (ux * g[4] + uz * g[5] - uy * g[8])
    gz = sqrt_three * g[3] + sqrt_fifteen * (uy * g[5] + ux * g[7]) + 3.0 * sqrt_five * uz * g[6]
    mixed = along - (gx * ux + gy * uy + gz * uz) * inv
    pick = (
        lax.broadcasted_iota(jnp.int32, (eb, CB), 0) // K
        == lax.broadcasted_iota(jnp.int32, (eb, CB), 1)
    ).astype(f32)
    for c, (gu, u) in enumerate(((gx, ux), (gy, uy), (gz, uz))):
        value = jnp.where(valid, gu * inv + u * mixed, 0.0)
        edge_s[c] = value
        center_ref[c] = jnp.dot(value, pick, precision=lax.Precision.HIGHEST)
    energy_ref[...] = jnp.dot(g[18], pick, precision=lax.Precision.HIGHEST)

    padded = part_ref.shape[1]
    row_iota = lax.broadcasted_iota(jnp.int32, (padded, eb), 0)
    lane_iota = lax.broadcasted_iota(jnp.int32, (128, eb), 0)
    part_ref[...] = jnp.zeros_like(part_ref)

    def scatter(b, carry):
        nbr = nbr_ref[pl.ds(b, 1), :]
        safe = jnp.where(nbr >= 0, nbr, 0)
        here = row_iota == safe // 128
        hot = jnp.where(lane_iota == safe % 128, 1.0, 0.0).astype(bf16)
        terms = []
        for c in range(3):
            value = edge_s[c, pl.ds(b, 1), :]
            high = value.astype(bf16).astype(f32)
            terms.append(jnp.where(here, high, 0.0).astype(bf16))
            terms.append(jnp.where(here, value - high, 0.0).astype(bf16))
        got = lax.dot_general(
            jnp.concatenate(terms, axis=0),
            hot,
            (((1,), (1,)), ((), ())),
            preferred_element_type=f32,
        )
        for c in range(3):
            part_ref[c] += (
                got[2 * c * padded : (2 * c + 1) * padded]
                + got[(2 * c + 1) * padded : (2 * c + 2) * padded]
            )
        return carry

    lax.fori_loop(0, hs, scatter, 0)


def kernel(
    rows, nbr, own, tab, lat, wp, sel_y, w1, wf, wh, v2, wb, wt, wl, sel_g, wo,
    out, part, center, energy, vec_s, feat_s, grad_s, edge_s,
):
    step = pl.program_id(0)

    @pl.when(step == 0)
    def _():
        geometry(rows, nbr, own, tab, vec_s, feat_s)

    network(step, lat, wp, sel_y, w1, wf, wh, v2, wb, wt, wl, sel_g, wo, feat_s, grad_s, out)

    @pl.when(step == pl.num_programs(0) - 1)
    def _():
        pull(rows, nbr, vec_s, grad_s, edge_s, part, center, energy)


def prepare(w_latent, w_tensor, w_radial, species_center, species_neighbor, w_hidden, w_update, w_out):
    tc = w_tensor.shape[0] // 3
    width = w_hidden.shape[0]
    we, wv, wlp = w_latent[:, :tc], w_latent[:, tc : 2 * tc], w_latent[:, 2 * tc :]
    wo_col = jnp.pad(w_out[:, None], ((0, 0), (0, 127)))
    wp = jnp.concatenate([we, we, wv, wv, wo_col], axis=1)
    sel_y = np.zeros((2 * FR, 128 * len(COLUMNS)), np.float32)
    for c, pair in enumerate(COLUMNS):
        for half, m in enumerate(pair):
            if m >= 0:
                sel_y[m, c * 128 + half * 64 : c * 128 + half * 64 + 64] = 1.0
    w1 = jnp.concatenate([wlp, w_tensor, w_tensor[2 * tc :]], axis=0)
    plain = jnp.concatenate(
        [
            jnp.zeros((9, width), f32),
            w_radial,
            jnp.zeros((1, width), f32),
            species_center,
            species_neighbor,
            jnp.zeros((FR - 28, width), f32),
        ],
        axis=0,
    )
    high = lax.reduce_precision(plain, 8, 7)
    wf = jnp.concatenate([high, plain - high], axis=0).astype(bf16)
    v2 = jnp.sum(w_update.astype(f32) * w_out.astype(f32)[None, :], axis=1)
    v2_high = lax.reduce_precision(v2, 8, 7)
    v2_mat = jnp.pad(jnp.stack([v2_high, v2 - v2_high], axis=1), ((0, 0), (0, 126))).astype(bf16)
    wb = (v2[:, None] * w_hidden.T.astype(f32)).astype(bf16)
    wt = jnp.concatenate([w_tensor, w_tensor[2 * tc :]], axis=0).T
    wl = jnp.concatenate([wlp.T, wv.T, wv.T, we.T, we.T], axis=0)
    fixed = np.zeros((128 * len(COLUMNS), FR), np.float32)
    for m in range(9):
        fixed[:, m] = sel_y[m]
    last = np.zeros((128, FR), np.float32)
    last[:, 17] = 1.0
    sel_g = jnp.concatenate(
        [
            jnp.asarray(fixed, bf16),
            jnp.pad(w_radial.T.astype(bf16), ((0, 0), (9, FR - 17))),
            jnp.asarray(last, bf16),
        ],
        axis=0,
    )
    return (
        wp, jnp.asarray(sel_y, bf16), w1, wf, w_hidden, v2_mat, wb, wt, wl, sel_g,
        w_out.astype(f32)[None, :],
    )


def run_device(nbr, own, tab, latents, weights):
    hs, eb, lat = latents.shape
    rows = tab.shape[1]
    padded = (rows + 7) // 8 * 8
    whole = lambda a: pl.BlockSpec(a.shape, lambda i, n=len(a.shape): (0,) * n)
    ops = (nbr, own, tab)
    block = pl.BlockSpec((TILE_BLOCKS, eb, lat), lambda i: (i, 0, 0))
    outs = (
        jax.ShapeDtypeStruct((hs, eb, lat), bf16),
        jax.ShapeDtypeStruct((3, padded, 128), f32),
        jax.ShapeDtypeStruct((3, hs, CB), f32),
        jax.ShapeDtypeStruct((hs, CB), f32),
    )
    return pl.pallas_call(
        functools.partial(kernel, rows),
        out_shape=outs,
        grid=(hs // TILE_BLOCKS,),
        in_specs=[whole(a) for a in ops] + [block] + [whole(a) for a in weights],
        out_specs=[block] + [whole(a) for a in outs[1:]],
        scratch_shapes=[
            pltpu.VMEM((3, hs, eb), f32),
            pltpu.VMEM((hs, FR, eb), f32),
            pltpu.VMEM((hs, FR, eb), f32),
            pltpu.VMEM((3, hs, eb), f32),
        ],
        compiler_params=pltpu.CompilerParams(vmem_limit_bytes=48 * 1024 * 1024),
        cost_estimate=pl.CostEstimate(
            flops=hs * eb * 1200000, bytes_accessed=4 * hs * eb * lat, transcendentals=0
        ),
    )(*ops, latents, *weights)


def per_device(
    positions, species, neighbors, migration, latents,
    w_latent, w_tensor, w_radial, species_center, species_neighbor, w_hidden, w_update, w_out,
):
    atom_count = positions.shape[-1]
    slot_count = migration.shape[-1]
    work_slots = slot_count // 2
    weights = prepare(
        w_latent, w_tensor, w_radial, species_center, species_neighbor, w_hidden, w_update, w_out
    )
    own_table = jnp.concatenate(
        [positions[0, 0, 0], species[0, 0, 0][None, :].astype(f32)], axis=0
    )
    sides = (("gx", 0), ("gy", 1), ("gz", 2))
    gathered = with_halo(own_table[None, None, None], sides, 1)
    table = gathered.transpose(3, 0, 1, 2, 4).reshape(4, 27 * atom_count // 128, 128)
    latent_grad, part, center, energy = run_device(
        neighbors[0, 0, 0],
        own_table.reshape(4, slot_count, CB),
        table,
        latents[0, 0, 0],
        weights,
    )
    rows = table.shape[1]
    region = -part[:, :rows].reshape(3, 27, atom_count)
    region = region.at[:, 13].add(center.reshape(3, atom_count))
    partial_value = region.transpose(1, 0, 2).reshape(3, 3, 3, 3, atom_count)
    padded = with_halo(partial_value.astype(bf16), sides, 1).astype(f32)
    home_force = padded[0::2, 0::2, 0::2].sum(axis=(0, 1, 2))
    moved = jnp.repeat(migration[0, 0, 0].astype(f32), CB)
    every = lax.all_gather(jnp.concatenate([home_force, moved[None]], axis=0), "gx")
    wanted = jnp.arange(work_slots * CB, dtype=jnp.int32)
    target = (lax.axis_index("gx") * work_slots + wanted // CB).astype(f32)
    inner = jnp.arange(atom_count, dtype=jnp.int32) % CB
    hot = (every[:, 3, :, None] == target) & (inner[:, None] == wanted % CB)
    forces = jnp.einsum(
        "dca,das->cs", every[:, :3], hot.astype(f32), precision=lax.Precision.HIGHEST
    )
    return (
        forces[None, None, None],
        energy.reshape(1, 1, 1, atom_count).astype(bf16),
        latent_grad[None, None, None],
    )


def solution(mesh):
    return jax.shard_map(
        per_device,
        mesh=mesh,
        in_specs=(
            P(("parts", "gx"), "gy", "gz", None, None),
            P(("parts", "gx"), "gy", "gz", None),
            P(("parts", "gx"), "gy", "gz", None, None),
            P(("parts", "gx"), "gy", "gz", None),
            P(("parts", "gx"), "gy", "gz", None, None, None),
            P(),
            P(),
            P(),
            P(),
            P(),
            P(),
            P(),
            P(),
        ),
        out_specs=(
            P(("parts", "gx"), "gy", "gz", None, None),
            P(("parts", "gx"), "gy", "gz", None),
            P(("parts", "gx"), "gy", "gz", None, None, None),
        ),
        check_vma=False,
    )
```

time: 579 us -> 133 us (0.23); the launches traced: 570 us -> 133 us
  waiting for transfers between devices: 200 us -> 15.2 us
  local copies, waits for them, and re-layouts: 115 us -> 13.5 us
  other arithmetic: 104 us -> 5.58 us
  matrix products: 79.8 us -> 0.37 us
  Pallas kernels: 0 us -> 58.5 us
  starting transfers between devices: 69 us -> 24.8 us
  blocking collectives: 0 us -> 13.4 us
    all_to_all x9 -> x0, waiting for transfers between devices: 198 us -> none  [the longest x1 88.3 us: per_device(): lax.all_to_all(answer_rows(work_latent_grad, arrived_marks), 'gx', split_...]
    dot_general x23 -> x1, matrix products: 79.8 us -> 0.37 us  [per_device(): jnp.einsum('dca,das->cs', every[:, :3], hot.astype(f32), precision=lax.Pr...]
    gather x19 -> x0, local copies, waits for them, and re-layouts: 60.1 us -> none  [the longest x2 32.8 us: per_device(): others = jnp.take(flat_table, safe_entry, axis=1)]
    pallas_call x0 -> x1, Pallas kernels: none -> 58.5 us  [run_device(): pl.pallas_call(functools.partial(kernel, rows), out_shape=outs, grid=(hs...]
    scatter-add x1, other arithmetic: 55.6 us -> 0.01 us  [per_device(): region = region.at[:, 13].add(center.reshape(3, atom_count))]
    all_to_all x9 -> x0, starting transfers between devices: 37.7 us -> none  [the longest x1 5.1 us: per_device(): lax.all_to_all(pack_rows(code_slots, source, filled), 'gx', split_axis=0,...]
    mul x15 -> x0, other arithmetic: 19.4 us -> none  [the longest x4 6.45 us: pack_rows(): return picked * row_mask(filled, picked)]
    reshape x13 -> x1, local copies, waits for them, and re-layouts: 15.2 us -> 0.06 us  [per_device(): gathered.transpose(3, 0, 1, 2, 4).reshape(4, 27 * atom_count // 128, 128)]
  transfers between devices with their start and end apart: 21 -> 12, of which waited for: 9 -> 7; matrix products, arithmetic and copies ran while one was open for 29% -> 11% of each run, Pallas kernels for 0% -> 0%
where the time goes in v1:
time: 133 us
  Pallas kernels  58.5 us (44%)
  starting transfers between devices  24.8 us (19%)
  waiting for transfers between devices  15.2 us (11%)
  local copies, waits for them, and re-layouts  13.5 us (10%)
  blocking collectives  13.4 us (10%)
  other arithmetic  5.58 us (4%)
    pallas_call x1, Pallas kernels, run_device(): pl.pallas_call(functools.partial(kernel, rows), out_shape=outs, grid=(hs...  58.5 us
    ppermute x6, starting transfers between devices, with_halo(): lax.ppermute(tail, axis, [(i, (i + 1) % count) for i in range(ends)])  17.1 us
    ppermute x6, waiting for transfers between devices, with_halo(): lax.ppermute(head, axis, [((i + 1) % count, i) for i in range(ends)])  14.9 us
    all_gather x1, blocking collectives, per_device(): lax.all_gather(jnp.concatenate([home_force, moved[None]], axis=0), 'gx')  13.4 us
    ppermute x6, starting transfers between devices, with_halo(): lax.ppermute(head, axis, [((i + 1) % count, i) for i in range(ends)])  7.75 us
    unnamed x26, local copies, waits for them, and re-layouts  5.85 us
  transfers between devices with their start and end apart: 12, of which 7 were waited for; matrix products, arithmetic and copies ran while one was open for 11% of the time, Pallas kernels for 0%

profile of v1, /device:TPU:0, one launch (start us, length us, event | category | flops | bytes accessed | tf_op | source)
XLA Modules:
  0.0 132.5 jit_solution(16900374930277635515)
XLA Ops:
  0.7 0.7 copy.99
  1.4 0.7 convert_bitcast_fusion.1
  2.1 4.9 %collective-permute-start = (f32[1,1,1,4,256]{4,3,2,1,0:T(4,128)S(1)}, f32[1,1,1,4,256]{4,3,2,1,0:T(4,128)S(1)}, u32[]{:S(2)}, u32[]{:S(2)}) collective-permute-start(f32[1,1,1,4,256]{4,3,2,1,0:T(4,128)S(1)} %maximum_bitcast_fusion.2), channel_id=1, source_target_pairs={{0,4},{4,8},{8,12},{1,5},{5,9},{9,13},{2,6},{6,10},{10,14},{3,7},{... | collective-permute-start | bytes 12296 | tf_op jit(solution)/shard_map/ppermute | solution.py:36
  7.1 1.3 collective-permute-start.1
  8.4 1.0 fusion.16
  9.4 0.9 slice.80
  10.3 0.1 copy.95
  10.4 1.0 copy.82
  11.4 0.1 pad_maximum_fusion
  11.5 0.1 maximum_bitcast_fusion.wt
  11.6 0.7 convert_element_type.96
  12.3 0.7 broadcast_in_dim.42
  13.0 0.8 slice.78
  13.9 0.7 convert_reduce_fusion.1
  14.8 0.7 convert_bitcast_fusion
  15.5 2.3 %concatenate.61 = f32[32,256]{1,0:T(8,128)S(1)} concatenate(f32[9,256]{1,0:T(8,128)S(1)} %broadcast_in_dim.35, f32[8,256]{1,0:T(8,128)} %param.25, f32[1,256]{1,0:T(1,128)S(1)} %broadcast_in_dim.36, f32[5,256]{1,0:T(8,128)} %param.26, f32[5,256]{1,0:T(8,128)} %param.27, f32[4,256]{1,0:T(4,128)S(1)} %broadcast_in_dim.37), dimensions={0} | concatenate | bytes 65536 | tf_op jit(solution)/shard_map/concatenate | solution.py:313
  17.8 1.0 multiply_reduce_fusion
  18.9 1.0 copy.84
  19.9 0.1 fusion.7.wb
  20.0 0.7 reduce.2
  20.9 0.1 fusion.4.wp
  21.1 3.4 %collective-permute-start.2 = (f32[3,1,1,4,256]{4,3,2,1,0:T(4,128)S(1)}, f32[3,1,1,4,256]{4,3,2,1,0:T(4,128)S(1)}, u32[]{:S(2)}, u32[]{:S(2)}) collective-permute-start(f32[3,1,1,4,256]{4,3,2,1,0:T(4,128)S(1)} %pad_maximum_fusion.13), channel_id=1, source_target_pairs={{0,2},{1,3},{4,6},{5,7},{8,10},{9,11},{12,14},{13,15},{16,18},{17,... | collective-permute-start | bytes 36872 | tf_op jit(solution)/shard_map/ppermute | solution.py:36
  24.5 1.3 collective-permute-start.3
  25.9 4.2 %collective-permute-done.3 = f32[3,1,1,4,256]{4,3,2,1,0:T(4,128)S(1)} collective-permute-done((f32[3,1,1,4,256]{4,3,2,1,0:T(4,128)S(1)}, f32[3,1,1,4,256]{4,3,2,1,0:T(4,128)S(1)}, u32[]{:S(2)}, u32[]{:S(2)}) %collective-permute-start.3) | collective-permute-done | bytes 12320 | tf_op jit(solution)/shard_map/ppermute | solution.py:38
  30.2 1.3 collective-permute-start.4
  31.5 1.3 collective-permute-start.5
  32.8 0.1 copy.86.w1
  32.9 0.1 copy.83
  33.0 0.2 copy.87.sel_g
  33.3 1.2 collective-permute-done.5
  34.7 2.2 %copy-done.1 = bf16[1,1,1,32,256,256]{5,4,3,2,1,0:T(8,128)(2,1)S(1)} copy-done((bf16[1,1,1,32,256,256]{5,4,3,2,1,0:T(8,128)(2,1)S(1)}, bf16[1,1,1,32,256,256]{5,4,3,2,1,0:T(8,128)(2,1)}, u32[]{:S(2)}) %copy-start.1) | copy-done | bytes 4194328
  36.9 58.5 %shard_map.175 = (bf16[32,256,256]{2,1,0:T(8,128)(2,1)}, f32[3,56,128]{2,1,0:T(8,128)S(1)}, f32[3,32,8]{2,1,0:T(8,128)S(1)}, f32[32,8]{1,0:T(8,128)S(1)}) custom-call(s32[32,256]{1,0:T(8,128)S(1)} %bitcast.47, f32[4,32,8]{2,1,0:T(8,128)S(1)} %pad_maximum_fusion.2.own, f32[4,54,128]{2,1,0:T(8,128)S(1)} %reshape.168.tab, bf16[32,256,256]{2,1,0:T(8,128)(2,1)S(1)} %bitcast.46, ...), custom_call_target="tpu_custom_call" | custom-call | flops 9830400000 | bytes 8388608 | tf_op jit(solution)/shard_map/pallas_call | solution.py:364
  95.7 4.5 %collective-permute-start.6 = (bf16[1,3,3,3,256]{4,3,2,1,0:T(4,128)(2,1)S(1)}, bf16[1,3,3,3,256]{4,3,2,1,0:T(4,128)(2,1)S(1)}, u32[]{:S(2)}, u32[]{:S(2)}) collective-permute-start(bf16[1,3,3,3,256]{4,3,2,1,0:T(4,128)(2,1)S(1)} %bitcast.52), channel_id=1, source_target_pairs={{0,4},{4,8},{8,12},{1,5},{5,9},{9,13},{2,6},{6,10},{10,14},{3,7},{... | collective-permute-start | bytes 41480 | tf_op jit(solution)/shard_map/ppermute | solution.py:36
  100.3 1.3 collective-permute-start.7
  101.6 0.1 broadcast_compare_fusion
  101.7 4.2 %collective-permute-done.7 = bf16[1,3,3,3,256]{4,3,2,1,0:T(4,128)(2,1)S(1)} collective-permute-done((bf16[1,3,3,3,256]{4,3,2,1,0:T(4,128)(2,1)S(1)}, bf16[1,3,3,3,256]{4,3,2,1,0:T(4,128)(2,1)S(1)}, u32[]{:S(2)}, u32[]{:S(2)}) %collective-permute-start.7) | collective-permute-done | bytes 13856 | tf_op jit(solution)/shard_map/ppermute | solution.py:38
  106.0 1.6 %collective-permute-start.8 = (bf16[5,1,3,3,256]{4,3,2,1,0:T(4,128)(2,1)S(1)}, bf16[5,1,3,3,256]{4,3,2,1,0:T(4,128)(2,1)S(1)}, u32[]{:S(2)}, u32[]{:S(2)}) collective-permute-start(bf16[5,1,3,3,256]{4,3,2,1,0:T(4,128)(2,1)S(1)} %get-tuple-element.39), channel_id=1, source_target_pairs={{0,2},{1,3},{4,6},{5,7},{8,10},{9,11},{12,14},{13,15},{16,18},{17,... | collective-permute-start | bytes 69128 | tf_op jit(solution)/shard_map/ppermute | solution.py:36
  107.6 1.3 collective-permute-start.9
  108.9 0.2 collective-permute-done.8
  109.2 4.2 %collective-permute-done.9 = bf16[5,1,3,3,256]{4,3,2,1,0:T(4,128)(2,1)S(1)} collective-permute-done((bf16[5,1,3,3,256]{4,3,2,1,0:T(4,128)(2,1)S(1)}, bf16[5,1,3,3,256]{4,3,2,1,0:T(4,128)(2,1)S(1)}, u32[]{:S(2)}, u32[]{:S(2)}) %collective-permute-start.9) | collective-permute-done | bytes 23072 | tf_op jit(solution)/shard_map/ppermute | solution.py:38
  113.5 1.3 collective-permute-start.10
  114.8 1.3 collective-permute-start.11
  116.3 0.7 convert_element_type.109
  116.9 1.0 collective-permute-done.11
  117.9 0.2 pad_maximum_fusion.1
  118.2 13.4 %all-gather.1 = f32[4,4,256]{2,1,0:T(4,128)S(1)} all-gather(f32[1,4,256]{2,1,0:T(4,128)S(1)} %maximum_bitcast_fusion.3), channel_id=2, replica_groups=mesh['parts'=2,'gx'=4,'gy'=2,'gz'=2] {'gx'}, dimensions={0}, use_global_device_ids=true | all-gather | bytes 20480 | tf_op jit(solution)/shard_map/all_gather | solution.py:413
  131.6 0.4 convolution_bitcast_fusion
  132.0 0.6 copy.90
  (65 shorter events, 1.4 us)
Async XLA Ops:
  0.6 20.4 %copy-start.4 = (bf16[768,32]{0,1:T(8,128)(2,1)S(1)}, bf16[768,32]{0,1:T(8,128)(2,1)}, u32[]{:S(2)}) copy-start(bf16[768,32]{0,1:T(8,128)(2,1)} %constant.91.clone) | copy-start | bytes 147460
  0.6 20.4 %copy-start.5 = (bf16[128,32]{0,1:T(8,128)(2,1)S(1)}, bf16[128,32]{0,1:T(8,128)(2,1)}, u32[]{:S(2)}) copy-start(bf16[128,32]{0,1:T(8,128)(2,1)} %constant.92.clone) | copy-start | bytes 24580
  0.7 34.1 %copy-start.3 = (bf16[64,768]{1,0:T(8,128)(2,1)S(1)}, bf16[64,768]{1,0:T(8,128)(2,1)}, u32[]{:S(2)}) copy-start(bf16[64,768]{1,0:T(8,128)(2,1)} %constant.93.clone.sel_y) | copy-start | bytes 294916
  0.7 34.0 %copy-start = (bf16[256,256]{1,0:T(8,128)(2,1)S(1)}, bf16[256,256]{1,0:T(8,128)(2,1)}, u32[]{:S(2)}) copy-start(bf16[256,256]{1,0:T(8,128)(2,1)} %wh.1) | copy-start | bytes 393220
  0.7 34.0 %copy-start.2 = (s32[1,1,1,32,256]{4,3,2,1,0:T(8,128)S(1)}, s32[1,1,1,32,256]{4,3,2,1,0:T(8,128)}, u32[]{:S(2)}) copy-start(s32[1,1,1,32,256]{4,3,2,1,0:T(8,128)} %param.20) | copy-start | bytes 98308
  2.1 19.0 %collective-permute-start = (f32[1,1,1,4,256]{4,3,2,1,0:T(4,128)S(1)}, f32[1,1,1,4,256]{4,3,2,1,0:T(4,128)S(1)}, u32[]{:S(2)}, u32[]{:S(2)}) collective-permute-start(f32[1,1,1,4,256]{4,3,2,1,0:T(4,128)S(1)} %maximum_bitcast_fusion.2), channel_id=1, source_target_pairs={{0,4},{4,8},{8,12},{1,5},{5,9},{9,13},{2,6},{6,10},{10,14},{3,7},{... | collective-permute-start | bytes 12296 | tf_op jit(solution)/shard_map/ppermute | solution.py:36
  7.1 14.1 %collective-permute-start.1 = (f32[1,1,1,4,256]{4,3,2,1,0:T(4,128)S(1)}, f32[1,1,1,4,256]{4,3,2,1,0:T(4,128)S(1)}, u32[]{:S(2)}, u32[]{:S(2)}) collective-permute-start(f32[1,1,1,4,256]{4,3,2,1,0:T(4,128)S(1)} %maximum_bitcast_fusion.2), channel_id=1, source_target_pairs={{4,0},{8,4},{12,8},{5,1},{9,5},{13,9},{6,2},{10,6},{14,10},{7,3},{... | collective-permute-start | bytes 12296 | tf_op jit(solution)/shard_map/ppermute | solution.py:38
  21.1 4.8 %collective-permute-start.2 = (f32[3,1,1,4,256]{4,3,2,1,0:T(4,128)S(1)}, f32[3,1,1,4,256]{4,3,2,1,0:T(4,128)S(1)}, u32[]{:S(2)}, u32[]{:S(2)}) collective-permute-start(f32[3,1,1,4,256]{4,3,2,1,0:T(4,128)S(1)} %pad_maximum_fusion.13), channel_id=1, source_target_pairs={{0,2},{1,3},{4,6},{5,7},{8,10},{9,11},{12,14},{13,15},{16,18},{17,... | collective-permute-start | bytes 36872 | tf_op jit(solution)/shard_map/ppermute | solution.py:36
  24.5 5.6 %collective-permute-start.3 = (f32[3,1,1,4,256]{4,3,2,1,0:T(4,128)S(1)}, f32[3,1,1,4,256]{4,3,2,1,0:T(4,128)S(1)}, u32[]{:S(2)}, u32[]{:S(2)}) collective-permute-start(f32[3,1,1,4,256]{4,3,2,1,0:T(4,128)S(1)} %pad_maximum_fusion.13), channel_id=1, source_target_pairs={{2,0},{3,1},{6,4},{7,5},{10,8},{11,9},{14,12},{15,13},{18,16},{19,... | collective-permute-start | bytes 36872 | tf_op jit(solution)/shard_map/ppermute | solution.py:38
  30.2 3.2 %collective-permute-start.4 = (f32[3,3,1,4,256]{4,3,2,1,0:T(4,128)S(1)}, f32[3,3,1,4,256]{4,3,2,1,0:T(4,128)S(1)}, u32[]{:S(2)}, u32[]{:S(2)}) collective-permute-start(f32[3,3,1,4,256]{4,3,2,1,0:T(4,128)S(1)} %pad_maximum_fusion.8), channel_id=1, source_target_pairs={{0,1},{2,3},{4,5},{6,7},{8,9},{10,11},{12,13},{14,15},{16,17},{18,... | collective-permute-start | bytes 110600 | tf_op jit(solution)/shard_map/ppermute | solution.py:36
  31.5 3.1 %collective-permute-start.5 = (f32[3,3,1,4,256]{4,3,2,1,0:T(4,128)S(1)}, f32[3,3,1,4,256]{4,3,2,1,0:T(4,128)S(1)}, u32[]{:S(2)}, u32[]{:S(2)}) collective-permute-start(f32[3,3,1,4,256]{4,3,2,1,0:T(4,128)S(1)} %pad_maximum_fusion.8), channel_id=1, source_target_pairs={{1,0},{3,2},{5,4},{7,6},{9,8},{11,10},{13,12},{15,14},{17,16},{19,... | collective-permute-start | bytes 110600 | tf_op jit(solution)/shard_map/ppermute | solution.py:38
  34.7 2.2 %copy-start.1 = (bf16[1,1,1,32,256,256]{5,4,3,2,1,0:T(8,128)(2,1)S(1)}, bf16[1,1,1,32,256,256]{5,4,3,2,1,0:T(8,128)(2,1)}, u32[]{:S(2)}) copy-start(bf16[1,1,1,32,256,256]{5,4,3,2,1,0:T(8,128)(2,1)} %param.22) | copy-start | bytes 12582916
  36.9 72.0 %copy-start.6 = (s32[1,1,1,32]{3,2,1,0:T(1,128)S(1)}, s32[1,1,1,32]{3,2,1,0:T(1,128)}, u32[]{:S(2)}) copy-start(s32[1,1,1,32]{3,2,1,0:T(1,128)} %param.21) | copy-start | bytes 388
  95.7 6.0 %collective-permute-start.6 = (bf16[1,3,3,3,256]{4,3,2,1,0:T(4,128)(2,1)S(1)}, bf16[1,3,3,3,256]{4,3,2,1,0:T(4,128)(2,1)S(1)}, u32[]{:S(2)}, u32[]{:S(2)}) collective-permute-start(bf16[1,3,3,3,256]{4,3,2,1,0:T(4,128)(2,1)S(1)} %bitcast.52), channel_id=1, source_target_pairs={{0,4},{4,8},{8,12},{1,5},{5,9},{9,13},{2,6},{6,10},{10,14},{3,7},{... | collective-permute-start | bytes 41480 | tf_op jit(solution)/shard_map/ppermute | solution.py:36
  100.3 5.7 %collective-permute-start.7 = (bf16[1,3,3,3,256]{4,3,2,1,0:T(4,128)(2,1)S(1)}, bf16[1,3,3,3,256]{4,3,2,1,0:T(4,128)(2,1)S(1)}, u32[]{:S(2)}, u32[]{:S(2)}) collective-permute-start(bf16[1,3,3,3,256]{4,3,2,1,0:T(4,128)(2,1)S(1)} %bitcast.51), channel_id=1, source_target_pairs={{4,0},{8,4},{12,8},{5,1},{9,5},{13,9},{6,2},{10,6},{14,10},{7,3},{... | collective-permute-start | bytes 41480 | tf_op jit(solution)/shard_map/ppermute | solution.py:38
  106.0 3.2 %collective-permute-start.8 = (bf16[5,1,3,3,256]{4,3,2,1,0:T(4,128)(2,1)S(1)}, bf16[5,1,3,3,256]{4,3,2,1,0:T(4,128)(2,1)S(1)}, u32[]{:S(2)}, u32[]{:S(2)}) collective-permute-start(bf16[5,1,3,3,256]{4,3,2,1,0:T(4,128)(2,1)S(1)} %get-tuple-element.39), channel_id=1, source_target_pairs={{0,2},{1,3},{4,6},{5,7},{8,10},{9,11},{12,14},{13,15},{16,18},{17,... | collective-permute-start | bytes 69128 | tf_op jit(solution)/shard_map/ppermute | solution.py:36
  107.6 5.8 %collective-permute-start.9 = (bf16[5,1,3,3,256]{4,3,2,1,0:T(4,128)(2,1)S(1)}, bf16[5,1,3,3,256]{4,3,2,1,0:T(4,128)(2,1)S(1)}, u32[]{:S(2)}, u32[]{:S(2)}) collective-permute-start(bf16[5,1,3,3,256]{4,3,2,1,0:T(4,128)(2,1)S(1)} %get-tuple-element.40), channel_id=1, source_target_pairs={{2,0},{3,1},{6,4},{7,5},{10,8},{11,9},{14,12},{15,13},{18,16},{19,... | collective-permute-start | bytes 69128 | tf_op jit(solution)/shard_map/ppermute | solution.py:38
  113.5 3.4 %collective-permute-start.10 = (bf16[5,5,1,3,256]{4,3,2,1,0:T(4,128)(2,1)S(1)}, bf16[5,5,1,3,256]{4,3,2,1,0:T(4,128)(2,1)S(1)}, u32[]{:S(2)}, u32[]{:S(2)}) collective-permute-start(bf16[5,5,1,3,256]{4,3,2,1,0:T(4,128)(2,1)S(1)} %get-tuple-element.37), channel_id=1, source_target_pairs={{0,1},{2,3},{4,5},{6,7},{8,9},{10,11},{12,13},{14,15},{16,17},{18,... | collective-permute-start | bytes 115208 | tf_op jit(solution)/shard_map/ppermute | solution.py:36
  114.8 3.1 %collective-permute-start.11 = (bf16[5,5,1,3,256]{4,3,2,1,0:T(4,128)(2,1)S(1)}, bf16[5,5,1,3,256]{4,3,2,1,0:T(4,128)(2,1)S(1)}, u32[]{:S(2)}, u32[]{:S(2)}) collective-permute-start(bf16[5,5,1,3,256]{4,3,2,1,0:T(4,128)(2,1)S(1)} %get-tuple-element.38), channel_id=1, source_target_pairs={{1,0},{3,2},{5,4},{7,6},{9,8},{11,10},{13,12},{15,14},{17,16},{19,... | collective-permute-start | bytes 115208 | tf_op jit(solution)/shard_map/ppermute | solution.py:38

commit v2 on v1

--- a/solution.py
+++ b/solution.py
@@ -25,21 +25,243 @@
 COLUMNS = ((0, 1), (-1, 2), (-1, 3), (4, 5), (6, 7), (8, -1))
 
 
-def with_halo(cells, sides, width):
-    for axis, dim in sides:
-        count = lax.axis_size(axis)
-        ends = count - 1
-        head = lax.slice_in_dim(cells, 0, width, axis=dim)
-        tail = lax.slice_in_dim(cells, cells.shape[dim] - width, cells.shape[dim], axis=dim)
-        cells = jnp.concatenate(
-            [
-                lax.ppermute(tail, axis, [(i, (i + 1) % count) for i in range(ends)]),
-                cells,
-                lax.ppermute(head, axis, [((i + 1) % count, i) for i in range(ends)]),
-            ],
-            axis=dim,
+def near_steps(sizes):
+    spans = [(-1, 0, 1) if n > 1 else (0,) for n in sizes]
+    steps = [(x, y, z) for x in spans[0] for y in spans[1] for z in spans[2]]
+    return [d for d in steps if d != (0, 0, 0)]
+
+
+def slot_sizes(sizes):
+    return tuple(min(n, 3) for n in sizes)
+
+
+def slot_of(sizes, here, step):
+    index = 0
+    for n, at, d in zip(sizes, here, step):
+        place = d + 1 if n >= 3 else (at + d if n == 2 else 0)
+        index = index * min(n, 3) + place
+    return index
+
+
+def inside(sizes, here, step):
+    ok = None
+    for n, at, d in zip(sizes, here, step):
+        part = None
+        if d == -1:
+            part = at > 0
+        elif d == 1:
+            part = at < n - 1
+        if part is not None:
+            ok = part if ok is None else jnp.logical_and(ok, part)
+    return ok
+
+
+def moved(here, step):
+    return {"gx": here[0] + step[0], "gy": here[1] + step[1], "gz": here[2] + step[2]}
+
+
+def beside(sizes, here):
+    spans = []
+    for n, at in zip(sizes, here):
+        low = jnp.where(at > 0, 1, 0) if n > 1 else 0
+        high = jnp.where(at < n - 1, 1, 0) if n > 1 else 0
+        spans.append(low + high + 1)
+    return spans
+
+
+def spread_kernel(sizes, own_ref, out_ref, send_sem, recv_sem):
+    here = tuple(lax.axis_index(n) for n in ("gx", "gy", "gz"))
+    steps = near_steps(sizes)
+    out_ref[...] = jnp.zeros_like(out_ref)
+    out_ref[slot_of(sizes, here, (0, 0, 0))] = own_ref[...]
+    barrier = pltpu.get_barrier_semaphore()
+    for d in steps:
+        @pl.when(inside(sizes, here, d))
+        def _(d=d):
+            pl.semaphore_signal(
+                barrier, inc=1, device_id=moved(here, d), device_id_type=pl.DeviceIdType.MESH
+            )
+    spans = beside(sizes, here)
+    pl.semaphore_wait(barrier, spans[0] * spans[1] * spans[2] - 1)
+
+    def copy(n, d):
+        back = tuple(-v for v in d)
+        there = tuple(h + v for h, v in zip(here, d))
+        return pltpu.make_async_remote_copy(
+            src_ref=own_ref,
+            dst_ref=out_ref.at[slot_of(sizes, there, back)],
+            send_sem=send_sem.at[n],
+            recv_sem=recv_sem.at[n],
+            device_id=moved(here, d),
+            device_id_type=pl.DeviceIdType.MESH,
         )
-    return cells
+
+    for n, d in enumerate(steps):
+        @pl.when(inside(sizes, here, d))
+        def _(n=n, d=d):
+            copy(n, d).start()
+    for n, d in enumerate(steps):
+        @pl.when(inside(sizes, here, d))
+        def _(n=n, d=d):
+            copy(n, d).wait_send()
+        back = tuple(-v for v in d)
+
+        @pl.when(inside(sizes, here, back))
+        def _(n=n, back=back):
+            pltpu.make_async_remote_copy(
+                src_ref=own_ref,
+                dst_ref=out_ref.at[slot_of(sizes, here, back)],
+                send_sem=send_sem.at[n],
+                recv_sem=recv_sem.at[n],
+                device_id=moved(here, back),
+                device_id_type=pl.DeviceIdType.MESH,
+            ).wait_recv()
+
+
+def collect_kernel(
+    sizes, part_ref, center_ref, mig_ref, out_ref, near_ref, far_ref, s1, r1, s2, r2
+):
+    here = tuple(lax.axis_index(n) for n in ("gx", "gy", "gz"))
+    steps = near_steps(sizes)
+    ring = sizes[0]
+    near_ref[...] = jnp.zeros_like(near_ref)
+    shifts = list(range(1, ring))
+
+    def peer(s):
+        return {"gx": lax.rem(here[0] + s, ring), "gy": here[1], "gz": here[2]}
+
+    barrier = pltpu.get_barrier_semaphore()
+    for d in steps:
+        @pl.when(inside(sizes, here, d))
+        def _(d=d):
+            pl.semaphore_signal(
+                barrier, inc=1, device_id=moved(here, d), device_id_type=pl.DeviceIdType.MESH
+            )
+    for gap in [g for g in range(1 - ring, ring) if abs(g) > 1]:
+        @pl.when(jnp.logical_and(here[0] + gap >= 0, here[0] + gap < ring))
+        def _(gap=gap):
+            pl.semaphore_signal(
+                barrier,
+                inc=1,
+                device_id=moved(here, (gap, 0, 0)),
+                device_id_type=pl.DeviceIdType.MESH,
+            )
+    spans = beside(sizes, here)
+    pl.semaphore_wait(barrier, spans[0] * spans[1] * spans[2] - 1 + ring - spans[0])
+
+    def give(n, d):
+        return pltpu.make_async_remote_copy(
+            src_ref=part_ref.at[slot_of(sizes, here, d)],
+            dst_ref=near_ref.at[n],
+            send_sem=s1.at[n],
+            recv_sem=r1.at[n],
+            device_id=moved(here, d),
+            device_id_type=pl.DeviceIdType.MESH,
+        )
+
+    for n, d in enumerate(steps):
+        @pl.when(inside(sizes, here, d))
+        def _(n=n, d=d):
+            give(n, d).start()
+    for n, d in enumerate(steps):
+        back = tuple(-v for v in d)
+
+        @pl.when(inside(sizes, here, back))
+        def _(n=n, back=back):
+            pltpu.make_async_remote_copy(
+                src_ref=center_ref,
+                dst_ref=near_ref.at[n],
+                send_sem=s1.at[n],
+                recv_sem=r1.at[n],
+                device_id=moved(here, back),
+                device_id_type=pl.DeviceIdType.MESH,
+            ).wait_recv()
+    force = center_ref[...] - part_ref[slot_of(sizes, here, (0, 0, 0))]
+    for n in range(len(steps)):
+        force = force - near_ref[n]
+    row = lax.broadcasted_iota(jnp.int32, force.shape, 0)
+    mig = mig_ref[...]
+    force = jnp.where(row == 6, mig[0:1], jnp.where(row == 7, mig[1:2], force))
+    far_ref[0] = force
+
+    def pass_on(s):
+        return pltpu.make_async_remote_copy(
+            src_ref=far_ref.at[0],
+            dst_ref=far_ref.at[s],
+            send_sem=s2.at[s],
+            recv_sem=r2.at[s],
+            device_id=peer(s),
+            device_id_type=pl.DeviceIdType.MESH,
+        )
+
+    for s in shifts:
+        pass_on(s).start()
+    slots = lax.broadcasted_iota(jnp.int32, (128, 128), 0)
+    lanes = lax.broadcasted_iota(jnp.int32, (128, 128), 1)
+    same = slots % CB == lanes % CB
+    target = (here[0] * (128 // CB) + slots // CB).astype(f32)
+    total = jnp.zeros((8, 128), f32)
+    for s in range(ring):
+        if s > 0:
+            pass_on(s).wait_recv()
+        block = far_ref[s]
+        for h in range(2):
+            hot = jnp.where((block[6 + h : 7 + h] == target) & same, 1.0, 0.0)
+            mine = jnp.where(row % 2 == h, block, 0.0)
+            total = total + lax.dot_general(
+                mine, hot, (((1,), (1,)), ((), ())), precision=lax.Precision.HIGHEST,
+                preferred_element_type=f32,
+            )
+    for c in range(3):
+        out_ref[c : c + 1, :] = total[2 * c : 2 * c + 1] + total[2 * c + 1 : 2 * c + 2]
+    for s in shifts:
+        pass_on(s).wait_send()
+    for n, d in enumerate(steps):
+        @pl.when(inside(sizes, here, d))
+        def _(n=n, d=d):
+            give(n, d).wait_send()
+
+
+def spread(own, sizes):
+    count = len(near_steps(sizes))
+    total = int(np.prod(slot_sizes(sizes)))
+    return pl.pallas_call(
+        functools.partial(spread_kernel, sizes),
+        out_shape=jax.ShapeDtypeStruct((total, 8, 128), f32),
+        in_specs=[pl.BlockSpec(memory_space=pltpu.VMEM)],
+        out_specs=pl.BlockSpec(memory_space=pltpu.VMEM),
+        scratch_shapes=[pltpu.SemaphoreType.DMA((count,)), pltpu.SemaphoreType.DMA((count,))],
+        compiler_params=pltpu.CompilerParams(collective_id=0, has_side_effects=True),
+    )(own)
+
+
+def collect(part, center, mig, sizes):
+    count = len(near_steps(sizes))
+    dma = pltpu.SemaphoreType.DMA
+    return pl.pallas_call(
+        functools.partial(collect_kernel, sizes),
+        out_shape=jax.ShapeDtypeStruct((3, 128), f32),
+        in_specs=[pl.BlockSpec(memory_space=pltpu.VMEM)] * 3,
+        out_specs=pl.BlockSpec(memory_space=pltpu.VMEM),
+        scratch_shapes=[
+            pltpu.VMEM((count, 8, 128), f32),
+            pltpu.VMEM((sizes[0], 8, 128), f32),
+            dma((count,)), dma((count,)), dma((sizes[0],)), dma((sizes[0],)),
+        ],
+        compiler_params=pltpu.CompilerParams(collective_id=1, has_side_effects=True),
+    )(part, center, mig)
+
+
+def places(sizes, nbr):
+    here = tuple(lax.axis_index(n) for n in ("gx", "gy", "gz"))
+    safe = jnp.where(nbr >= 0, nbr, 0)
+    region = safe // 256
+    step = (region // 9 - 1, region // 3 % 3 - 1, region % 3 - 1)
+    slot = 0
+    for n, at, d in zip(sizes, here, step):
+        place = d + 1 if n >= 3 else (at + d if n == 2 else 0)
+        slot = slot * min(n, 3) + place
+    return slot, safe // 128 % 2, safe % 128
 
 
 def sin_cos(angle):
@@ -70,7 +292,7 @@
     return jnp.dot(a, b, preferred_element_type=f32)
 
 
-def geometry(rows, nbr_ref, own_ref, tab_ref, vec_s, feat_s):
+def geometry(sizes, nbr_ref, own_ref, tab_ref, vec_s, feat_s, code_s):
     hs, eb = nbr_ref.shape
     lane = lax.broadcasted_iota(jnp.int32, (hs, eb), 1)
     atom = lane // K
@@ -83,24 +305,30 @@
         centers.append(acc)
     nbr = nbr_ref[...]
     valid = nbr >= 0
-    safe = jnp.where(valid, nbr, 0)
-    row_of = safe // 128
-    lane_of = safe % 128
+    slot, half, lane_of = places(sizes, nbr)
+    row_of = slot * 2 + half
+    code_s[0] = slot
+    code_s[1] = half
+    code_s[2] = lane_of
     halves = eb // 128
 
     def look(q, acc):
-        out = []
-        for c in range(4):
-            src = jnp.broadcast_to(tab_ref[c, pl.ds(q, 1), :], (hs, 128))
-            for h in range(halves):
-                got = jnp.take_along_axis(
-                    src, lane_of[:, h * 128 : (h + 1) * 128], axis=1, mode="promise_in_bounds"
-                )
-                out.append(jnp.where(row_of[:, h * 128 : (h + 1) * 128] == q, got, acc[c * halves + h]))
+        out = list(acc)
+        for k in range(2):
+            for c in range(4):
+                src = jnp.broadcast_to(tab_ref[q, pl.ds(2 * c + k, 1), :], (hs, 128))
+                for h in range(halves):
+                    cols = slice(h * 128, (h + 1) * 128)
+                    got = jnp.take_along_axis(
+                        src, lane_of[:, cols], axis=1, mode="promise_in_bounds"
+                    )
+                    out[c * halves + h] = jnp.where(
+                        row_of[:, cols] == 2 * q + k, got, out[c * halves + h]
+                    )
         return tuple(out)
 
     found = lax.fori_loop(
-        0, rows, look, tuple(jnp.zeros((hs, 128), f32) for _ in range(4 * halves))
+        0, tab_ref.shape[0], look, tuple(jnp.zeros((hs, 128), f32) for _ in range(4 * halves))
     )
     others = [jnp.concatenate(found[c * halves : (c + 1) * halves], axis=1) for c in range(4)]
     safe_vec = (2.0 * cutoff_radius, 0.0, 0.0)
@@ -211,7 +439,7 @@
     out_ref[...] = glat.astype(bf16).reshape(out_ref.shape)
 
 
-def pull(rows, nbr_ref, vec_s, grad_s, edge_s, part_ref, center_ref, energy_ref):
+def pull(nbr_ref, vec_s, grad_s, edge_s, code_s, part_ref, center_ref):
     hs, eb = nbr_ref.shape
     valid = nbr_ref[...] >= 0
     x, y, z = vec_s[0], vec_s[1], vec_s[2]
@@ -239,130 +467,139 @@
     gy = sqrt_three * g[2] + sqrt_fifteen * (ux * g[4] + uz * g[5] - uy * g[8])
     gz = sqrt_three * g[3] + sqrt_fifteen * (uy * g[5] + ux * g[7]) + 3.0 * sqrt_five * uz * g[6]
     mixed = along - (gx * ux + gy * uy + gz * uz) * inv
-    pick = (
-        lax.broadcasted_iota(jnp.int32, (eb, CB), 0) // K
-        == lax.broadcasted_iota(jnp.int32, (eb, CB), 1)
-    ).astype(f32)
     for c, (gu, u) in enumerate(((gx, ux), (gy, uy), (gz, uz))):
         value = jnp.where(valid, gu * inv + u * mixed, 0.0)
         edge_s[c] = value
-        center_ref[c] = jnp.dot(value, pick, precision=lax.Precision.HIGHEST)
-    energy_ref[...] = jnp.dot(g[18], pick, precision=lax.Precision.HIGHEST)
-
-    padded = part_ref.shape[1]
-    row_iota = lax.broadcasted_iota(jnp.int32, (padded, eb), 0)
+    edge_s[3] = g[18]
+
+    count = part_ref.shape[0]
+    row = lax.broadcasted_iota(jnp.int32, (8, eb), 0)
     lane_iota = lax.broadcasted_iota(jnp.int32, (128, eb), 0)
+    atom = lax.broadcasted_iota(jnp.int32, (128, eb), 1) // K
+    per_half = hs // 2
     part_ref[...] = jnp.zeros_like(part_ref)
+    center_ref[...] = jnp.zeros_like(center_ref)
+
+    def across(values, hot):
+        got = lax.dot_general(
+            values.astype(bf16), hot, (((1,), (1,)), ((), ())), preferred_element_type=f32
+        )
+        mid = got.shape[0] // 2
+        return got[:mid] + got[mid:]
 
     def scatter(b, carry):
-        nbr = nbr_ref[pl.ds(b, 1), :]
-        safe = jnp.where(nbr >= 0, nbr, 0)
-        here = row_iota == safe // 128
-        hot = jnp.where(lane_iota == safe % 128, 1.0, 0.0).astype(bf16)
-        terms = []
+        slot, half, lane = (code_s[c, pl.ds(b, 1), :] for c in range(3))
+        hot = jnp.where(lane_iota == lane, 1.0, 0.0).astype(bf16)
+        own_hot = jnp.where(lane_iota == b % per_half * CB + atom, 1.0, 0.0).astype(bf16)
+        value = edge_s[3, pl.ds(b, 1), :]
+        value = jnp.broadcast_to(value, (8, eb))
         for c in range(3):
-            value = edge_s[c, pl.ds(b, 1), :]
-            high = value.astype(bf16).astype(f32)
-            terms.append(jnp.where(here, high, 0.0).astype(bf16))
-            terms.append(jnp.where(here, value - high, 0.0).astype(bf16))
-        got = lax.dot_general(
-            jnp.concatenate(terms, axis=0),
-            hot,
-            (((1,), (1,)), ((), ())),
-            preferred_element_type=f32,
+            value = jnp.where(row // 2 == c, edge_s[c, pl.ds(b, 1), :], value)
+        high = value.astype(bf16).astype(f32)
+        low = value - high
+        own = row % 2 == b // per_half
+        center_ref[...] += across(
+            jnp.concatenate([jnp.where(own, high, 0.0), jnp.where(own, low, 0.0)], axis=0),
+            own_hot,
         )
-        for c in range(3):
-            part_ref[c] += (
-                got[2 * c * padded : (2 * c + 1) * padded]
-                + got[(2 * c + 1) * padded : (2 * c + 2) * padded]
-            )
+        there = row % 2 == half
+        high = jnp.where(there, high, 0.0)
+        low = jnp.where(there, low, 0.0)
+        terms = [jnp.where(slot == q, high, 0.0) for q in range(count)]
+        terms += [jnp.where(slot == q, low, 0.0) for q in range(count)]
+        part_ref[...] += across(jnp.concatenate(terms, axis=0), hot).reshape(part_ref.shape)
         return carry
 
     lax.fori_loop(0, hs, scatter, 0)
 
 
+def prepare(wlat, wten, wrad, wcen, wnei, whid, wupd, wout, sel, wp, w1, wf, v2, wb, wt, wl, sel_g, plain_s):
+    tc = wten.shape[0] // 3
+    wide = wlat[...].astype(f32)
+    first, rest = wide[:, : 2 * tc], wide[:, 2 * tc :]
+    turned = jnp.concatenate([first[:, tc:], first[:, :tc]], axis=1)
+    lane = lax.broadcasted_iota(jnp.int32, first.shape, 1)
+    we = jnp.where(lane < tc, first, turned)
+    wv = jnp.where(lane < tc, turned, first)
+    out_row = wout[...].astype(f32)
+    wp[:, 0:128] = we.astype(bf16)
+    wp[:, 128:256] = wv.astype(bf16)
+    wp[:, 256:384] = jnp.broadcast_to(out_row, (128, out_row.shape[1])).T.astype(bf16)
+    n = wide.shape[0]
+    w1[0:n] = wlat[:, 2 * tc :]
+    w1[n : n + 3 * tc] = wten[...]
+    w1[n + 3 * tc : n + 4 * tc] = wten[2 * tc :]
+    wl[0:n] = rest.T.astype(bf16)
+    wl[n : n + 128] = wv.T.astype(bf16)
+    wl[n + 128 : n + 256] = we.T.astype(bf16)
+    ten = wten[...].astype(f32)
+    wt[...] = jnp.concatenate([ten, ten[2 * tc :]], axis=0).T.astype(bf16)
+    plain_s[...] = jnp.zeros_like(plain_s)
+    plain_s[9:17] = wrad[...]
+    sel_g[0 : sel.shape[0]] = sel[...].astype(bf16)
+    at = sel.shape[0]
+    sel_g[at : at + n] = plain_s[...].T.astype(bf16)
+    tail = lax.broadcasted_iota(jnp.int32, (128, FR), 1)
+    sel_g[at + n : at + n + 128] = jnp.where(tail == 17, 1.0, 0.0).astype(bf16)
+    plain_s[18:23] = wcen[...]
+    plain_s[23:28] = wnei[...]
+    plain = plain_s[...]
+    high = plain.astype(bf16).astype(f32)
+    wf[0:FR] = high.astype(bf16)
+    wf[FR : 2 * FR] = (plain - high).astype(bf16)
+    col = jnp.sum(wupd[...].astype(f32) * out_row, axis=1, keepdims=True)
+    col_high = col.astype(bf16).astype(f32)
+    lane = lax.broadcasted_iota(jnp.int32, (n, 128), 1)
+    v2[...] = jnp.where(
+        lane == 0, col_high, jnp.where(lane == 1, col - col_high, 0.0)
+    ).astype(bf16)
+    wb[...] = (col * whid[...].astype(f32).T).astype(bf16)
+
+
 def kernel(
-    rows, nbr, own, tab, lat, wp, sel_y, w1, wf, wh, v2, wb, wt, wl, sel_g, wo,
-    out, part, center, energy, vec_s, feat_s, grad_s, edge_s,
+    sizes, nbr, own, tab, lat, sel_y, sel, wlat, wten, wrad, wcen, wnei, whid, wupd, wout,
+    out, part, center,
+    vec_s, feat_s, grad_s, edge_s, code_s, wp, w1, wf, v2, wb, wt, wl, sel_g, wo, plain_s,
 ):
     step = pl.program_id(0)
 
     @pl.when(step == 0)
     def _():
-        geometry(rows, nbr, own, tab, vec_s, feat_s)
-
-    network(step, lat, wp, sel_y, w1, wf, wh, v2, wb, wt, wl, sel_g, wo, feat_s, grad_s, out)
+        prepare(
+            wlat, wten, wrad, wcen, wnei, whid, wupd, wout, sel,
+            wp, w1, wf, v2, wb, wt, wl, sel_g, plain_s,
+        )
+        wo[...] = wout[...].astype(f32)
+        geometry(sizes, nbr, own, tab, vec_s, feat_s, code_s)
+
+    network(step, lat, wp, sel_y, w1, wf, whid, v2, wb, wt, wl, sel_g, wo, feat_s, grad_s, out)
 
     @pl.when(step == pl.num_programs(0) - 1)
     def _():
-        pull(rows, nbr, vec_s, grad_s, edge_s, part, center, energy)
-
-
-def prepare(w_latent, w_tensor, w_radial, species_center, species_neighbor, w_hidden, w_update, w_out):
-    tc = w_tensor.shape[0] // 3
-    width = w_hidden.shape[0]
-    we, wv, wlp = w_latent[:, :tc], w_latent[:, tc : 2 * tc], w_latent[:, 2 * tc :]
-    wo_col = jnp.pad(w_out[:, None], ((0, 0), (0, 127)))
-    wp = jnp.concatenate([we, we, wv, wv, wo_col], axis=1)
-    sel_y = np.zeros((2 * FR, 128 * len(COLUMNS)), np.float32)
+        pull(nbr, vec_s, grad_s, edge_s, code_s, part, center)
+
+
+def run_device(nbr, own, tab, latents, weights, sizes):
+    hs, eb, lat = latents.shape
+    whole = lambda a: pl.BlockSpec(a.shape, lambda i, n=len(a.shape): (0,) * n)
+    ops = (nbr, own, tab)
+    wide = 128 * len(COLUMNS)
+    sel_y = np.zeros((2 * FR, wide), np.float32)
     for c, pair in enumerate(COLUMNS):
         for half, m in enumerate(pair):
             if m >= 0:
                 sel_y[m, c * 128 + half * 64 : c * 128 + half * 64 + 64] = 1.0
-    w1 = jnp.concatenate([wlp, w_tensor, w_tensor[2 * tc :]], axis=0)
-    plain = jnp.concatenate(
-        [
-            jnp.zeros((9, width), f32),
-            w_radial,
-            jnp.zeros((1, width), f32),
-            species_center,
-            species_neighbor,
-            jnp.zeros((FR - 28, width), f32),
-        ],
-        axis=0,
-    )
-    high = lax.reduce_precision(plain, 8, 7)
-    wf = jnp.concatenate([high, plain - high], axis=0).astype(bf16)
-    v2 = jnp.sum(w_update.astype(f32) * w_out.astype(f32)[None, :], axis=1)
-    v2_high = lax.reduce_precision(v2, 8, 7)
-    v2_mat = jnp.pad(jnp.stack([v2_high, v2 - v2_high], axis=1), ((0, 0), (0, 126))).astype(bf16)
-    wb = (v2[:, None] * w_hidden.T.astype(f32)).astype(bf16)
-    wt = jnp.concatenate([w_tensor, w_tensor[2 * tc :]], axis=0).T
-    wl = jnp.concatenate([wlp.T, wv.T, wv.T, we.T, we.T], axis=0)
-    fixed = np.zeros((128 * len(COLUMNS), FR), np.float32)
-    for m in range(9):
-        fixed[:, m] = sel_y[m]
-    last = np.zeros((128, FR), np.float32)
-    last[:, 17] = 1.0
-    sel_g = jnp.concatenate(
-        [
-            jnp.asarray(fixed, bf16),
-            jnp.pad(w_radial.T.astype(bf16), ((0, 0), (9, FR - 17))),
-            jnp.asarray(last, bf16),
-        ],
-        axis=0,
-    )
-    return (
-        wp, jnp.asarray(sel_y, bf16), w1, wf, w_hidden, v2_mat, wb, wt, wl, sel_g,
-        w_out.astype(f32)[None, :],
-    )
-
-
-def run_device(nbr, own, tab, latents, weights):
-    hs, eb, lat = latents.shape
-    rows = tab.shape[1]
-    padded = (rows + 7) // 8 * 8
-    whole = lambda a: pl.BlockSpec(a.shape, lambda i, n=len(a.shape): (0,) * n)
-    ops = (nbr, own, tab)
+    fixed = np.zeros((wide, FR), np.float32)
+    fixed[:, :9] = sel_y[:9].T
+    weights = (jnp.asarray(sel_y, bf16), jnp.asarray(fixed, bf16)) + weights
     block = pl.BlockSpec((TILE_BLOCKS, eb, lat), lambda i: (i, 0, 0))
     outs = (
         jax.ShapeDtypeStruct((hs, eb, lat), bf16),
-        jax.ShapeDtypeStruct((3, padded, 128), f32),
-        jax.ShapeDtypeStruct((3, hs, CB), f32),
-        jax.ShapeDtypeStruct((hs, CB), f32),
+        jax.ShapeDtypeStruct(tab.shape, f32),
+        jax.ShapeDtypeStruct((8, 128), f32),
     )
     return pl.pallas_call(
-        functools.partial(kernel, rows),
+        functools.partial(kernel, sizes),
         out_shape=outs,
         grid=(hs // TILE_BLOCKS,),
         in_specs=[whole(a) for a in ops] + [block] + [whole(a) for a in weights],
@@ -371,7 +608,18 @@
             pltpu.VMEM((3, hs, eb), f32),
             pltpu.VMEM((hs, FR, eb), f32),
             pltpu.VMEM((hs, FR, eb), f32),
-            pltpu.VMEM((3, hs, eb), f32),
+            pltpu.VMEM((4, hs, eb), f32),
+            pltpu.VMEM((3, hs, eb), jnp.int32),
+            pltpu.VMEM((lat, 384), bf16),
+            pltpu.VMEM((2 * lat, lat), bf16),
+            pltpu.VMEM((2 * FR, lat), bf16),
+            pltpu.VMEM((lat, 128), bf16),
+            pltpu.VMEM((lat, lat), bf16),
+            pltpu.VMEM((lat, lat), bf16),
+            pltpu.VMEM((2 * lat, lat), bf16),
+            pltpu.VMEM((wide + lat + 128, FR), bf16),
+            pltpu.VMEM((1, lat), f32),
+            pltpu.VMEM((FR, lat), f32),
         ],
         compiler_params=pltpu.CompilerParams(vmem_limit_bytes=48 * 1024 * 1024),
         cost_estimate=pl.CostEstimate(
@@ -386,41 +634,28 @@
 ):
     atom_count = positions.shape[-1]
     slot_count = migration.shape[-1]
-    work_slots = slot_count // 2
-    weights = prepare(
-        w_latent, w_tensor, w_radial, species_center, species_neighbor, w_hidden, w_update, w_out
+    sizes = tuple(lax.axis_size(n) for n in ("gx", "gy", "gz"))
+    weights = (
+        w_latent, w_tensor, w_radial, species_center, species_neighbor, w_hidden, w_update,
+        w_out[None, :],
     )
     own_table = jnp.concatenate(
         [positions[0, 0, 0], species[0, 0, 0][None, :].astype(f32)], axis=0
     )
-    sides = (("gx", 0), ("gy", 1), ("gz", 2))
-    gathered = with_halo(own_table[None, None, None], sides, 1)
-    table = gathered.transpose(3, 0, 1, 2, 4).reshape(4, 27 * atom_count // 128, 128)
-    latent_grad, part, center, energy = run_device(
+    table = spread(own_table.reshape(8, 128), sizes)
+    latent_grad, part, center = run_device(
         neighbors[0, 0, 0],
         own_table.reshape(4, slot_count, CB),
         table,
         latents[0, 0, 0],
         weights,
-    )
-    rows = table.shape[1]
-    region = -part[:, :rows].reshape(3, 27, atom_count)
-    region = region.at[:, 13].add(center.reshape(3, atom_count))
-    partial_value = region.transpose(1, 0, 2).reshape(3, 3, 3, 3, atom_count)
-    padded = with_halo(partial_value.astype(bf16), sides, 1).astype(f32)
-    home_force = padded[0::2, 0::2, 0::2].sum(axis=(0, 1, 2))
-    moved = jnp.repeat(migration[0, 0, 0].astype(f32), CB)
-    every = lax.all_gather(jnp.concatenate([home_force, moved[None]], axis=0), "gx")
-    wanted = jnp.arange(work_slots * CB, dtype=jnp.int32)
-    target = (lax.axis_index("gx") * work_slots + wanted // CB).astype(f32)
-    inner = jnp.arange(atom_count, dtype=jnp.int32) % CB
-    hot = (every[:, 3, :, None] == target) & (inner[:, None] == wanted % CB)
-    forces = jnp.einsum(
-        "dca,das->cs", every[:, :3], hot.astype(f32), precision=lax.Precision.HIGHEST
-    )
+        sizes,
+    )
+    mig = jnp.broadcast_to(migration[0, 0, 0].astype(f32)[:, None], (slot_count, CB))
+    forces = collect(part, center, mig.reshape(2, 128), sizes)
     return (
         forces[None, None, None],
-        energy.reshape(1, 1, 1, atom_count).astype(bf16),
+        center[6:8].reshape(1, 1, 1, atom_count).astype(bf16),
         latent_grad[None, None, None],
     )
 

time: 133 us -> 95.4 us (0.72)
  starting transfers between devices: 24.8 us -> 0 us
  Pallas kernels: 58.5 us -> 73.9 us
  waiting for transfers between devices: 15.2 us -> 0 us
  blocking collectives: 13.4 us -> 0 us
  local copies, waits for them, and re-layouts: 13.5 us -> 17.2 us
  other arithmetic: 5.58 us -> 2.81 us
    ppermute x12 -> x0, starting transfers between devices: 24.8 us -> none  [the longest x6 17.1 us: with_halo(): lax.ppermute(tail, axis, [(i, (i + 1) % count) for i in range(ends)])]
    pallas_call x1 -> x3, Pallas kernels: 58.5 us -> 73.9 us  [the longest x1 52.7 us: run_device(): pl.pallas_call(functools.partial(kernel, sizes), out_shape=outs, grid=(hs...]
    ppermute x12 -> x0, waiting for transfers between devices: 15.2 us -> none  [the longest x6 14.9 us: with_halo(): lax.ppermute(head, axis, [((i + 1) % count, i) for i in range(ends)])]
    all_gather x1 -> x0, blocking collectives: 13.4 us -> none  [per_device(): lax.all_gather(jnp.concatenate([home_force, moved[None]], axis=0), 'gx')]
    unnamed x26 -> x32, local copies, waits for them, and re-layouts: 5.85 us -> 14.4 us
    slice x6 -> x1, local copies, waits for them, and re-layouts: 2.79 us -> 0.01 us  [per_device(): center[6:8].reshape(1, 1, 1, atom_count).astype(bf16)]
    concatenate x3 -> x0, local copies, waits for them, and re-layouts: 2.67 us -> none  [the longest x1 2.32 us: prepare(): jnp.concatenate([jnp.zeros((9, width), f32), w_radial, jnp.zeros((1, widt...]
    convert_element_type x8 -> x1, other arithmetic: 1.52 us -> 0.02 us  [per_device(): migration[0, 0, 0].astype(f32)[:, None]]
  transfers between devices with their start and end apart: 12 -> 0, of which waited for: 7 -> 0; matrix products, arithmetic and copies ran while one was open for 11% -> 0% of each run, Pallas kernels for 0% -> 0%
where the time goes in v2:
time: 95.4 us; the launch traced here: 94.6 us
  Pallas kernels  73.9 us (77%)
  local copies, waits for them, and re-layouts  17.2 us (18%)
  other arithmetic  2.81 us (3%)
    pallas_call x1, Pallas kernels, run_device(): pl.pallas_call(functools.partial(kernel, sizes), out_shape=outs, grid=(hs...  52.7 us
    unnamed x32, local copies, waits for them, and re-layouts  14.4 us
    pallas_call x1, Pallas kernels, collect(): pl.pallas_call(functools.partial(collect_kernel, sizes), out_shape=jax.Sh...  12.3 us
    pallas_call x1, Pallas kernels, spread(): pl.pallas_call(functools.partial(spread_kernel, sizes), out_shape=jax.Sha...  8.89 us

profile of v2, /device:TPU:0, one launch (start us, length us, event | category | flops | bytes accessed | tf_op | source)
XLA Modules:
  0.0 94.6 jit_solution(7677892061517435015)
XLA Ops:
  0.6 0.7 reduce
  1.3 0.1 concatenate.8
  1.4 0.7 convert_reduce_fusion
  2.1 0.1 convert_element_type.47
  2.2 0.7 copy.27
  2.9 0.7 convert_bitcast_fusion
  3.6 0.6 reshape.61.own_ref
  4.2 8.9 %shard_map.166.tab = f32[12,8,128]{2,1,0:T(8,128)} custom-call(f32[8,128]{1,0:T(8,128)} %reshape.61.own_ref), custom_call_target="tpu_custom_call" | custom-call | tf_op jit(solution)/shard_map/pallas_call | solution.py:228
  13.1 0.7 broadcast_in_dim.17.wout
  13.8 0.0 copy-start.1
  13.8 0.8 copy-done.1
  14.6 0.0 copy-start.3
  14.6 2.2 %copy-done.3 = bf16[1,1,1,32,256,256]{5,4,3,2,1,0:T(8,128)(2,1)S(1)} copy-done((bf16[1,1,1,32,256,256]{5,4,3,2,1,0:T(8,128)(2,1)S(1)}, bf16[1,1,1,32,256,256]{5,4,3,2,1,0:T(8,128)(2,1)}, u32[]{:S(2)}) %copy-start.3) | copy-done | bytes 4194328
  16.8 0.0 copy-start.4
  16.8 0.9 copy-done.4
  17.7 0.0 copy-start.5
  17.7 0.9 copy-done.5
  18.6 0.0 copy-start.6
  18.6 0.9 copy-done.6
  19.5 0.0 copy-start.7
  19.5 0.9 copy-done.7
  20.4 0.0 copy-start.8
  20.4 0.8 copy-done.8
  21.2 0.0 copy-start.9
  21.2 0.7 copy-done.9
  21.9 0.0 copy-start.10
  21.9 0.7 copy-done.10
  22.6 0.0 copy-start.11
  22.6 0.7 copy-done.11
  23.2 0.0 copy-start.12
  23.3 0.9 copy-done.12
  24.2 0.0 copy-start.13
  24.2 0.9 copy-done.13
  25.1 0.0 copy-start.14
  25.1 52.7 %shard_map.167 = (bf16[32,256,256]{2,1,0:T(8,128)(2,1)}, f32[12,8,128]{2,1,0:T(8,128)S(1)}, f32[8,128]{1,0:T(8,128)S(1)}) custom-call(s32[32,256]{1,0:T(8,128)S(1)} %bitcast.10, f32[4,32,8]{2,1,0:T(8,128)S(1)} %pad_maximum_fusion.own, f32[12,8,128]{2,1,0:T(8,128)S(1)} %copy-done.1, bf16[32,256,256]{2,1,0:T(8,128)(2,1)S(1)} %bitcast.9, ...), custom_call_target="tpu_custom_call" | custom-call | flops 9830400000 | bytes 8388608 | tf_op jit(solution)/shard_map/pallas_call | solution.py:601
  77.7 0.0 copy-start
  77.7 0.6 copy-done
  78.3 0.0 copy-start.2
  78.4 0.6 copy-done.2
  78.9 0.0 copy-done.14
  79.0 0.1 convert_element_type.50
  79.0 0.1 broadcast_in_dim.18
  79.1 0.7 broadcast_in_dim.19.mig_ref
  79.8 12.3 %shard_map.168 = f32[3,128]{1,0:T(4,128)} custom-call(f32[12,8,128]{2,1,0:T(8,128)} %copy-done, f32[8,128]{1,0:T(8,128)} %copy-done.2, f32[2,128]{1,0:T(2,128)} %broadcast_in_dim.19.mig_ref), custom_call_target="tpu_custom_call" | custom-call | tf_op jit(solution)/shard_map/pallas_call | solution.py:241
  92.1 1.2 %copy.24 = f32[1,1,1,3,128]{4,2,3,1,0:T(1,128)} copy(f32[1,1,1,3,128]{4,3,2,1,0:T(4,128)} %bitcast.12) | data formatting | bytes 3072
  93.3 0.7 convert.3
  94.0 0.6 convert_element_type.51
  (4 shorter events, 0.1 us)
Async XLA Ops:
  13.8 0.8 copy-start.1
  14.6 2.2 %copy-start.3 = (bf16[1,1,1,32,256,256]{5,4,3,2,1,0:T(8,128)(2,1)S(1)}, bf16[1,1,1,32,256,256]{5,4,3,2,1,0:T(8,128)(2,1)}, u32[]{:S(2)}) copy-start(bf16[1,1,1,32,256,256]{5,4,3,2,1,0:T(8,128)(2,1)} %param.19) | copy-start | bytes 12582916
  16.8 0.9 copy-start.4
  17.7 0.9 copy-start.5
  18.6 0.9 copy-start.6
  19.5 0.9 copy-start.7
  20.4 0.8 copy-start.8
  21.2 0.7 copy-start.9
  21.9 0.7 copy-start.10
  22.6 0.7 copy-start.11
  23.2 0.9 copy-start.12
  24.2 0.9 copy-start.13
  25.1 53.9 %copy-start.14 = (s32[1,1,1,32]{3,2,1,0:T(1,128)S(1)}, s32[1,1,1,32]{3,2,1,0:T(1,128)}, u32[]{:S(2)}) copy-start(s32[1,1,1,32]{3,2,1,0:T(1,128)} %param.18) | copy-start | bytes 388
  77.7 0.6 copy-start
  78.3 0.6 copy-start.2

commit v3 on v2

--- a/solution.py
+++ b/solution.py
@@ -12,7 +12,7 @@
 CB = 8
 K = 32
 FR = 32
-TILE_BLOCKS = 2
+TILE_BLOCKS = 4
 
 cutoff_radius = 6.0
 sqrt_three = 3.0**0.5
@@ -69,10 +69,14 @@
     return spans
 
 
-def spread_kernel(sizes, own_ref, out_ref, send_sem, recv_sem):
+def spread_kernel(sizes, pos_ref, kind_ref, out_ref, own_ref, send_sem, recv_sem):
     here = tuple(lax.axis_index(n) for n in ("gx", "gy", "gz"))
     steps = near_steps(sizes)
     out_ref[...] = jnp.zeros_like(out_ref)
+    for c in range(4):
+        line = pos_ref[c : c + 1, :] if c < 3 else kind_ref[...].astype(f32)
+        for h in range(2):
+            own_ref[2 * c + h : 2 * c + h + 1, :] = line[:, h * 128 : (h + 1) * 128]
     out_ref[slot_of(sizes, here, (0, 0, 0))] = own_ref[...]
     barrier = pltpu.get_barrier_semaphore()
     for d in steps:
@@ -180,8 +184,20 @@
     for n in range(len(steps)):
         force = force - near_ref[n]
     row = lax.broadcasted_iota(jnp.int32, force.shape, 0)
-    mig = mig_ref[...]
-    force = jnp.where(row == 6, mig[0:1], jnp.where(row == 7, mig[1:2], force))
+    hs = mig_ref.shape[1]
+    kept = lax.broadcasted_iota(jnp.int32, (8, hs), 1) // (hs // 2) == (
+        lax.broadcasted_iota(jnp.int32, (8, hs), 0) % 2
+    )
+    mig = jnp.where(kept, mig_ref[...].astype(f32), 0.0)
+    widen = (
+        lax.broadcasted_iota(jnp.int32, (hs, 128), 1) // CB
+        == lax.broadcasted_iota(jnp.int32, (hs, 128), 0) % (hs // 2)
+    )
+    mig = jnp.dot(
+        mig, jnp.where(widen, 1.0, 0.0), precision=lax.Precision.HIGHEST,
+        preferred_element_type=f32,
+    )
+    force = jnp.where(row >= 6, mig, force)
     far_ref[0] = force
 
     def pass_on(s):
@@ -222,17 +238,21 @@
             give(n, d).wait_send()
 
 
-def spread(own, sizes):
+def spread(pos, kind, sizes):
     count = len(near_steps(sizes))
     total = int(np.prod(slot_sizes(sizes)))
     return pl.pallas_call(
         functools.partial(spread_kernel, sizes),
         out_shape=jax.ShapeDtypeStruct((total, 8, 128), f32),
-        in_specs=[pl.BlockSpec(memory_space=pltpu.VMEM)],
+        in_specs=[pl.BlockSpec(memory_space=pltpu.VMEM)] * 2,
         out_specs=pl.BlockSpec(memory_space=pltpu.VMEM),
-        scratch_shapes=[pltpu.SemaphoreType.DMA((count,)), pltpu.SemaphoreType.DMA((count,))],
+        scratch_shapes=[
+            pltpu.VMEM((8, 128), f32),
+            pltpu.SemaphoreType.DMA((count,)),
+            pltpu.SemaphoreType.DMA((count,)),
+        ],
         compiler_params=pltpu.CompilerParams(collective_id=0, has_side_effects=True),
-    )(own)
+    )(pos, kind)
 
 
 def collect(part, center, mig, sizes):
@@ -292,17 +312,30 @@
     return jnp.dot(a, b, preferred_element_type=f32)
 
 
-def geometry(sizes, nbr_ref, own_ref, tab_ref, vec_s, feat_s, code_s):
+def geometry(sizes, nbr_ref, tab_ref, vec_s, feat_s, code_s):
     hs, eb = nbr_ref.shape
-    lane = lax.broadcasted_iota(jnp.int32, (hs, eb), 1)
-    atom = lane // K
+    here = tuple(lax.axis_index(n) for n in ("gx", "gy", "gz"))
+    own = tab_ref[slot_of(sizes, here, (0, 0, 0))]
+    block = lax.broadcasted_iota(jnp.int32, (hs, 128), 0)
+    lane = lax.broadcasted_iota(jnp.int32, (hs, 128), 1)
+    per_half = hs // 2
     centers = []
     for c in range(4):
-        own = own_ref[c]
-        acc = jnp.broadcast_to(own[:, 0:1], (hs, eb))
-        for a in range(1, CB):
-            acc = jnp.where(atom == a, own[:, a : a + 1], acc)
-        centers.append(acc)
+        src = jnp.where(block < per_half, own[2 * c : 2 * c + 1], own[2 * c + 1 : 2 * c + 2])
+        centers.append(
+            jnp.concatenate(
+                [
+                    jnp.take_along_axis(
+                        src,
+                        block % per_half * CB + (h * 128 + lane) // K,
+                        axis=1,
+                        mode="promise_in_bounds",
+                    )
+                    for h in range(eb // 128)
+                ],
+                axis=1,
+            )
+        )
     nbr = nbr_ref[...]
     valid = nbr >= 0
     slot, half, lane_of = places(sizes, nbr)
@@ -328,7 +361,11 @@
         return tuple(out)
 
     found = lax.fori_loop(
-        0, tab_ref.shape[0], look, tuple(jnp.zeros((hs, 128), f32) for _ in range(4 * halves))
+        0,
+        tab_ref.shape[0],
+        look,
+        tuple(jnp.zeros((hs, 128), f32) for _ in range(4 * halves)),
+        unroll=2 if tab_ref.shape[0] % 2 == 0 else 1,
     )
     others = [jnp.concatenate(found[c * halves : (c + 1) * halves], axis=1) for c in range(4)]
     safe_vec = (2.0 * cutoff_radius, 0.0, 0.0)
@@ -401,10 +438,12 @@
     ea_b = ys[3] * envs[3] + ys[4] * envs[4] + ys[5] * envs[5]
     inv = jnp.concatenate([(vw * ea_a).astype(bf16), (vw * ea_b).astype(bf16)], axis=1)
     p1 = dot(jnp.concatenate([lat, inv], axis=1), w1[...]) + dot(feat_low, wf[...])
+    p1 = p1.astype(bf16)
     s1 = sigmoid(p1)
     h1 = p1 * s1
     d1 = s1 + h1 * (1.0 - s1)
     p2 = dot(h1.astype(bf16), wh[...])
+    p2 = p2.astype(bf16)
     s2 = sigmoid(p2)
     h2 = p2 * s2
     d2 = s2 + h2 * (1.0 - s2)
@@ -510,7 +549,7 @@
         part_ref[...] += across(jnp.concatenate(terms, axis=0), hot).reshape(part_ref.shape)
         return carry
 
-    lax.fori_loop(0, hs, scatter, 0)
+    lax.fori_loop(0, hs, scatter, 0, unroll=4)
 
 
 def prepare(wlat, wten, wrad, wcen, wnei, whid, wupd, wout, sel, wp, w1, wf, v2, wb, wt, wl, sel_g, plain_s):
@@ -557,7 +596,7 @@
 
 
 def kernel(
-    sizes, nbr, own, tab, lat, sel_y, sel, wlat, wten, wrad, wcen, wnei, whid, wupd, wout,
+    sizes, nbr, tab, lat, sel_y, sel, wlat, wten, wrad, wcen, wnei, whid, wupd, wout,
     out, part, center,
     vec_s, feat_s, grad_s, edge_s, code_s, wp, w1, wf, v2, wb, wt, wl, sel_g, wo, plain_s,
 ):
@@ -570,7 +609,7 @@
             wp, w1, wf, v2, wb, wt, wl, sel_g, plain_s,
         )
         wo[...] = wout[...].astype(f32)
-        geometry(sizes, nbr, own, tab, vec_s, feat_s, code_s)
+        geometry(sizes, nbr, tab, vec_s, feat_s, code_s)
 
     network(step, lat, wp, sel_y, w1, wf, whid, v2, wb, wt, wl, sel_g, wo, feat_s, grad_s, out)
 
@@ -579,10 +618,10 @@
         pull(nbr, vec_s, grad_s, edge_s, code_s, part, center)
 
 
-def run_device(nbr, own, tab, latents, weights, sizes):
+def run_device(nbr, tab, latents, weights, sizes):
     hs, eb, lat = latents.shape
     whole = lambda a: pl.BlockSpec(a.shape, lambda i, n=len(a.shape): (0,) * n)
-    ops = (nbr, own, tab)
+    ops = (nbr, tab)
     wide = 128 * len(COLUMNS)
     sel_y = np.zeros((2 * FR, wide), np.float32)
     for c, pair in enumerate(COLUMNS):
@@ -621,7 +660,7 @@
             pltpu.VMEM((1, lat), f32),
             pltpu.VMEM((FR, lat), f32),
         ],
-        compiler_params=pltpu.CompilerParams(vmem_limit_bytes=48 * 1024 * 1024),
+        compiler_params=pltpu.CompilerParams(vmem_limit_bytes=62 * 1024 * 1024),
         cost_estimate=pl.CostEstimate(
             flops=hs * eb * 1200000, bytes_accessed=4 * hs * eb * lat, transcendentals=0
         ),
@@ -633,26 +672,20 @@
     w_latent, w_tensor, w_radial, species_center, species_neighbor, w_hidden, w_update, w_out,
 ):
     atom_count = positions.shape[-1]
-    slot_count = migration.shape[-1]
     sizes = tuple(lax.axis_size(n) for n in ("gx", "gy", "gz"))
     weights = (
         w_latent, w_tensor, w_radial, species_center, species_neighbor, w_hidden, w_update,
         w_out[None, :],
     )
-    own_table = jnp.concatenate(
-        [positions[0, 0, 0], species[0, 0, 0][None, :].astype(f32)], axis=0
-    )
-    table = spread(own_table.reshape(8, 128), sizes)
+    table = spread(positions[0, 0, 0], species[0, 0], sizes)
     latent_grad, part, center = run_device(
         neighbors[0, 0, 0],
-        own_table.reshape(4, slot_count, CB),
         table,
         latents[0, 0, 0],
         weights,
         sizes,
     )
-    mig = jnp.broadcast_to(migration[0, 0, 0].astype(f32)[:, None], (slot_count, CB))
-    forces = collect(part, center, mig.reshape(2, 128), sizes)
+    forces = collect(part, center, migration[0, 0], sizes)
     return (
         forces[None, None, None],
         center[6:8].reshape(1, 1, 1, atom_count).astype(bf16),

time: 95.4 us -> 73.3 us (0.77)
  local copies, waits for them, and re-layouts: 17.2 us -> 4.3 us
  Pallas kernels: 73.9 us -> 67.3 us
  other arithmetic: 2.81 us -> 0.69 us
    unnamed x32 -> x2, local copies, waits for them, and re-layouts: 14.4 us -> 2.5 us
    pallas_call x1, Pallas kernels: 52.7 us -> 46 us  [run_device(): pl.pallas_call(functools.partial(kernel, sizes), out_shape=outs, grid=(hs...]
    convert_element_type x3 -> x0, other arithmetic: 1.4 us -> none  [the longest x2 1.38 us: per_device(): species[0, 0, 0][None, :].astype(f32)]
where the time goes in v3:
time: 73.3 us; the launch traced here: 73 us
  Pallas kernels  67.3 us (92%)
  local copies, waits for them, and re-layouts  4.3 us (6%)
    pallas_call x1, Pallas kernels, run_device(): pl.pallas_call(functools.partial(kernel, sizes), out_shape=outs, grid=(hs...  46 us
    pallas_call x1, Pallas kernels, collect(): pl.pallas_call(functools.partial(collect_kernel, sizes), out_shape=jax.Sh...  12.5 us
    pallas_call x1, Pallas kernels, spread(): pl.pallas_call(functools.partial(spread_kernel, sizes), out_shape=jax.Sha...  8.91 us
    unnamed x2, local copies, waits for them, and re-layouts  2.5 us

profile of v3, /device:TPU:0, one launch (start us, length us, event | category | flops | bytes accessed | tf_op | source)
XLA Modules:
  0.0 73.0 jit_solution(16511254630597623701)
XLA Ops:
  0.6 1.2 %broadcast_in_dim.9.wout = bf16[1,256]{1,0:T(2,128)(2,1)} reshape(bf16[256]{0:T(256)(128)(2,1)} %param.27) | data formatting | bytes 1024 | tf_op jit(solution)/shard_map/broadcast_in_dim | solution.py:678
  1.9 1.3 %copy.21 = f32[1,1,1,3,256]{4,3,2,1,0:T(4,128)} copy(f32[1,1,1,3,256]{4,2,3,1,0:T(1,128)} %param.15) | data formatting | bytes 6144
  3.1 8.9 %shard_map.166.tab = f32[12,8,128]{2,1,0:T(8,128)} custom-call(f32[3,256]{1,0:T(4,128)} %bitcast.9, s32[1,256]{1,0:T(1,128)} %bitcast.11), custom_call_target="tpu_custom_call" | custom-call | tf_op jit(solution)/shard_map/pallas_call | solution.py:244
  12.0 46.0 %shard_map.167 = (bf16[32,256,256]{2,1,0:T(8,128)(2,1)}, f32[12,8,128]{2,1,0:T(8,128)}, f32[8,128]{1,0:T(8,128)}) custom-call(s32[32,256]{1,0:T(8,128)} %bitcast.14, f32[12,8,128]{2,1,0:T(8,128)} %shard_map.166.tab, bf16[32,256,256]{2,1,0:T(8,128)(2,1)} %bitcast.13, bf16[64,768]{1,0:T(8,128)(2,1)} %constant.4.clone.sel_y, ...), custom_call_target="tpu_custom_call" | custom-call | flops 9830400000 | bytes 8388608 | tf_op jit(solution)/shard_map/pallas_call | solution.py:640
  58.0 12.5 %shard_map.168 = f32[3,128]{1,0:T(4,128)} custom-call(f32[12,8,128]{2,1,0:T(8,128)} %get-tuple-element.6.part_ref, f32[8,128]{1,0:T(8,128)} %get-tuple-element.7.center_ref, s32[1,32]{1,0:T(1,128)} %bitcast.12), custom_call_target="tpu_custom_call" | custom-call | tf_op jit(solution)/shard_map/pallas_call | solution.py:261
  70.5 0.7 convert.3
  71.2 1.2 %copy.18 = f32[1,1,1,3,128]{4,2,3,1,0:T(1,128)} copy(f32[1,1,1,3,128]{4,3,2,1,0:T(4,128)} %bitcast.10) | data formatting | bytes 3072
  72.4 0.6 convert_element_type.12
  (1 shorter events, 0.0 us)

commit v4 on v3

--- a/solution.py
+++ b/solution.py
@@ -597,7 +597,7 @@
 
 def kernel(
     sizes, nbr, tab, lat, sel_y, sel, wlat, wten, wrad, wcen, wnei, whid, wupd, wout,
-    out, part, center,
+    out, part, center, energy,
     vec_s, feat_s, grad_s, edge_s, code_s, wp, w1, wf, v2, wb, wt, wl, sel_g, wo, plain_s,
 ):
     step = pl.program_id(0)
@@ -616,6 +616,7 @@
     @pl.when(step == pl.num_programs(0) - 1)
     def _():
         pull(nbr, vec_s, grad_s, edge_s, code_s, part, center)
+        energy[...] = jnp.concatenate([center[6:7], center[7:8]], axis=1).astype(bf16)
 
 
 def run_device(nbr, tab, latents, weights, sizes):
@@ -636,6 +637,7 @@
         jax.ShapeDtypeStruct((hs, eb, lat), bf16),
         jax.ShapeDtypeStruct(tab.shape, f32),
         jax.ShapeDtypeStruct((8, 128), f32),
+        jax.ShapeDtypeStruct((1, hs * CB), bf16),
     )
     return pl.pallas_call(
         functools.partial(kernel, sizes),
@@ -675,10 +677,10 @@
     sizes = tuple(lax.axis_size(n) for n in ("gx", "gy", "gz"))
     weights = (
         w_latent, w_tensor, w_radial, species_center, species_neighbor, w_hidden, w_update,
-        w_out[None, :],
+        w_out.astype(f32).reshape(1, -1),
     )
     table = spread(positions[0, 0, 0], species[0, 0], sizes)
-    latent_grad, part, center = run_device(
+    latent_grad, part, center, energy = run_device(
         neighbors[0, 0, 0],
         table,
         latents[0, 0, 0],
@@ -688,7 +690,7 @@
     forces = collect(part, center, migration[0, 0], sizes)
     return (
         forces[None, None, None],
-        center[6:8].reshape(1, 1, 1, atom_count).astype(bf16),
+        energy.reshape(1, 1, 1, atom_count),
         latent_grad[None, None, None],
     )
 

time: 73.3 us -> 72 us (0.982)
  local copies, waits for them, and re-layouts: 4.3 us -> 2.5 us
    broadcast_in_dim x1 -> x0, local copies, waits for them, and re-layouts: 1.22 us -> none  [per_device(): w_out[None, :]]
    reshape x0 -> x1, other arithmetic: none -> 1.22 us  [per_device(): w_out.astype(f32).reshape(1, -1)]
where the time goes in v4:
time: 72 us; the launch traced here: 71.7 us
  Pallas kernels  67.4 us (94%)
  local copies, waits for them, and re-layouts  2.5 us (3%)
  other arithmetic  1.22 us (2%)
    pallas_call x1, Pallas kernels, run_device(): pl.pallas_call(functools.partial(kernel, sizes), out_shape=outs, grid=(hs...  46 us
    pallas_call x1, Pallas kernels, collect(): pl.pallas_call(functools.partial(collect_kernel, sizes), out_shape=jax.Sh...  12.5 us
    pallas_call x1, Pallas kernels, spread(): pl.pallas_call(functools.partial(spread_kernel, sizes), out_shape=jax.Sha...  8.91 us
    unnamed x2, local copies, waits for them, and re-layouts  2.5 us

profile of v4, /device:TPU:0, one launch (start us, length us, event | category | flops | bytes accessed | tf_op | source)
XLA Modules:
  0.0 71.7 jit_solution(3237779676734210073)
XLA Ops:
  0.6 1.2 %reshape.17 = f32[256]{0:T(256)} convert(bf16[256]{0:T(256)(128)(2,1)} %param.27) | non-fusion elementwise | flops 256 | bytes 1536 | tf_op jit(solution)/shard_map/reshape | solution.py:680
  1.8 1.3 %copy.21 = f32[1,1,1,3,256]{4,3,2,1,0:T(4,128)} copy(f32[1,1,1,3,256]{4,2,3,1,0:T(1,128)} %param.15) | data formatting | bytes 6144
  3.1 8.9 %shard_map.166.tab = f32[12,8,128]{2,1,0:T(8,128)} custom-call(f32[3,256]{1,0:T(4,128)} %bitcast.11, s32[1,256]{1,0:T(1,128)} %bitcast.13), custom_call_target="tpu_custom_call" | custom-call | tf_op jit(solution)/shard_map/pallas_call | solution.py:244
  12.0 46.0 %shard_map.167 = (bf16[32,256,256]{2,1,0:T(8,128)(2,1)}, f32[12,8,128]{2,1,0:T(8,128)}, f32[8,128]{1,0:T(8,128)}, bf16[1,256]{1,0:T(2,128)(2,1)}) custom-call(s32[32,256]{1,0:T(8,128)} %bitcast.16, f32[12,8,128]{2,1,0:T(8,128)} %shard_map.166.tab, bf16[32,256,256]{2,1,0:T(8,128)(2,1)} %bitcast.15, bf16[64,768]{1,0:T(8,128)(2,1)} %constant.4.clone.sel_y, ...), custom_call_target="tpu_custom_call" | custom-call | flops 9830400000 | bytes 8388608 | tf_op jit(solution)/shard_map/pallas_call | solution.py:642
  58.0 12.5 %shard_map.168 = f32[3,128]{1,0:T(4,128)} custom-call(f32[12,8,128]{2,1,0:T(8,128)} %get-tuple-element.7.part_ref, f32[8,128]{1,0:T(8,128)} %get-tuple-element.8.center_ref, s32[1,32]{1,0:T(1,128)} %bitcast.14), custom_call_target="tpu_custom_call" | custom-call | tf_op jit(solution)/shard_map/pallas_call | solution.py:261
  70.5 1.2 %copy.18 = f32[1,1,1,3,128]{4,2,3,1,0:T(1,128)} copy(f32[1,1,1,3,128]{4,3,2,1,0:T(4,128)} %bitcast.12) | data formatting | bytes 3072
